TPU v7x, 256 devices: a whole 4x4x8 slice. The times are simulated.
256 devices in a mesh: dp: 64 (over x, z_lo, y, core), mp: 4 (over z_hi).
Axes of the slice: x: 4, y: 4, z: 8 (z_hi: 4, z_lo: 2; z = z_hi * 2 + z_lo), core: 2. Of those that a mesh axis runs over, the one named last changes fastest.
Arguments:
- attn_out: bfloat16 [65536, 1024], P('dp'), may hold values from -16 to 16
- out_grad: bfloat16 [65536, 8192], P('dp', 'mp'), may hold values from -0.078125 to 0.078125
- left_old: float32 [1024, 1024], P('dp'), may hold values from -6 to 6
- right_old: float32 [4, 2048, 2048], P('mp', 'dp'), may hold values from -6 to 6
- basis: bfloat16 [4, 2048, 2048], P('mp', 'dp'), may hold values from -0.125 to 0.125
Outputs:
- left_new: float32 [1024, 1024], P('dp')
- right_new: float32 [4, 2048, 2048], P('mp', 'dp')
- rotated: bfloat16 [1024, 8192], P('dp', 'mp')
All inputs are finite; a program needn't handle non-finite values.
Results may differ from a plain program's by a relative error of at most 0.003.
The roundings to bfloat16 on the way count: a program that leaves them out, or rounds other values in their place, can miss the bound.
Values may be sent and summed in bfloat16 or wider, within the bound.
A program may use at most 64 MiB of HBM per device.

v0:
```python
import jax
import jax.numpy as jnp
from jax import lax
from jax.sharding import PartitionSpec as P


def body(attn_out, out_grad, left_old, right_old, basis):
    rows_dev = left_old.shape[0]
    block_cols = out_grad.shape[1]
    columns_all = block_cols * lax.axis_size("mp")
    whole_rows = rows_dev * lax.axis_size("dp")
    grad = lax.psum_scatter(
        jnp.einsum("tr,tc->rc", attn_out, out_grad, preferred_element_type=jnp.float32),
        "dp",
        scatter_dimension=0,
        tiled=True,
    )
    grad_b = grad.astype(jnp.bfloat16)
    partial_gram = jnp.einsum(
        "ic,jc->ij",
        grad_b,
        lax.all_gather(grad_b, "dp", axis=0, tiled=True),
        preferred_element_type=jnp.float32,
    )
    total = lax.psum(partial_gram, "mp")
    left_new = 0.9 * left_old + 0.1 * (total / columns_all)
    columns = lax.all_to_all(grad_b, "dp", split_axis=1, concat_axis=0, tiled=True)
    right_gram = jnp.einsum(
        "ik,il->kl",
        columns,
        lax.all_gather(columns, "dp", axis=1, tiled=True),
        preferred_element_type=jnp.float32,
    )
    right_new = 0.9 * right_old + 0.1 * (right_gram / whole_rows)[None]
    basis_rows = basis[0]
    rotated = lax.psum_scatter(
        jnp.dot(columns, basis_rows, preferred_element_type=jnp.float32),
        "dp",
        scatter_dimension=0,
        tiled=True,
    ).astype(jnp.bfloat16)
    return (left_new, right_new, rotated)


def solution(mesh):
    return jax.shard_map(
        body,
        mesh=mesh,
        in_specs=(
            P("dp", None),
            P("dp", "mp"),
            P("dp", None),
            P("mp", "dp", None),
            P("mp", "dp", None),
        ),
        out_specs=(P("dp", None), P("mp", "dp", None), P("dp", "mp")),
        check_vma=False,
    )
```

profile of v0, /device:TPU:1, one launch (start us, length us, event | category | flops | bytes accessed | tf_op | source)
XLA Modules:
  0.0 895.6 jit_solution(2457596443853806563)
XLA Ops:
  7.2 0.0 copy-start
  7.2 0.0 reduce-scatter.3.cloned.1.call-start
  7.2 1.5 copy-done
  8.8 8.9 fusion.4
  17.7 0.0 reduce-scatter.3.cloned.1.call-update
  17.7 0.0 copy-start.2
  17.7 0.0 all-gather.3.cloned.1.call-start
  17.8 298.9 %reduce-scatter.3.cloned.1.call-done = f32[16,2048]{1,0:T(8,128)} async-done(((f32[1024,2048]{1,0:T(8,128)}), f32[16,2048]{1,0:T(8,128)}) %reduce-scatter.3.cloned.1.call-update) | async-done | bytes 131088 | tf_op jit(solution)/shard_map/reduce_scatter | solution.py:12
  316.7 1.5 convert_element_type.6
  318.2 0.0 all-gather.3.cloned.1.call-update
  318.2 1.1 all_to_all.14
  319.3 0.2 copy.12
  319.5 0.8 reshape.10
  320.3 10.3 %all-to-all-start = ((bf16[64,2,256]{2,1,0:T(2,128)(2,1)}), bf16[64,2,256]{2,1,0:T(2,128)(2,1)S(1)}, u32[]{:S(2)}, u32[]{:S(2)}) async-start(bf16[64,2,256]{2,1,0:T(2,128)(2,1)} %reshape.10), calls=%async_computation.1 | async-start | bytes 131072 | tf_op jit(solution)/shard_map/all_to_all | solution.py:27
  330.6 0.0 all-reduce.2.cloned.1.call-start
  330.6 98.3 %all-gather.3.cloned.1.call-done = bf16[1024,2048]{1,0:T(8,128)(2,1)} async-done(((bf16[16,2048]{1,0:T(8,128)(2,1)}), bf16[1024,2048]{1,0:T(8,128)(2,1)}) %all-gather.3.cloned.1.call-update) | async-done | bytes 4194320 | tf_op jit(solution)/shard_map/all_gather | solution.py:22
  428.9 4.1 fusion.5
  433.0 0.0 all-reduce.2.cloned.1.call-update
  433.0 0.0 all-gather.5.cloned.1.call-start
  433.1 0.0 all-to-all-done
  433.1 0.2 reshape.11
  433.3 0.8 copy.10
  434.0 0.0 all-gather.5.cloned.1.call-update
  434.1 0.0 reduce-scatter.5.cloned.1.call-start
  434.1 0.0 copy-done.2
  434.1 4.4 fusion.2
  438.6 0.0 copy-start.3
  438.6 0.0 copy-start.1
  438.6 0.0 reduce-scatter.5.cloned.1.call-update
  438.6 40.4 %all-reduce.2.cloned.1.call-done = f32[16,1024]{1,0:T(8,128)} async-done(((f32[16,1024]{1,0:T(8,128)}), f32[16,1024]{1,0:T(8,128)}) %all-reduce.2.cloned.1.call-update) | async-done | bytes 65552 | tf_op jit(solution)/shard_map/psum | solution.py:25
  479.0 0.0 copy-done.3
  479.0 1.5 multiply_add_fusion
  480.4 110.5 %all-gather.5.cloned.1.call-done = bf16[1024,2048]{0,1:T(8,128)(2,1)} async-done(((bf16[1024,32]{0,1:T(8,128)(2,1)}), bf16[1024,2048]{0,1:T(8,128)(2,1)}) %all-gather.5.cloned.1.call-update) | async-done | bytes 4194320 | tf_op jit(solution)/shard_map/all_gather | solution.py:31
  590.9 0.0 copy-done.1
  590.9 4.3 fusion.1
  595.2 292.4 %reduce-scatter.5.cloned.1.call-done = f32[16,2048]{1,0:T(8,128)} async-done(((f32[1024,2048]{1,0:T(8,128)}), f32[16,2048]{1,0:T(8,128)}) %reduce-scatter.5.cloned.1.call-update) | async-done | bytes 131088 | tf_op jit(solution)/shard_map/reduce_scatter | solution.py:36
  887.6 1.5 convert_element_type.7
Async XLA Ops:
  7.2 1.6 copy-start
  7.2 309.5 %reduce-scatter.3.cloned.1.call-start = ((), (), s32[]{:S(2)}) async-start(), calls=%async_computation.3 | async-start | bytes 8519680 | tf_op jit(solution)/shard_map/reduce_scatter | solution.py:12
  17.7 416.4 %copy-start.2 = (bf16[1,32,2048]{2,1,0:T(8,128)(2,1)S(1)}, bf16[1,32,2048]{2,1,0:T(8,128)(2,1)}, u32[]{:S(2)}) copy-start(bf16[1,32,2048]{2,1,0:T(8,128)(2,1)} %param.9) | copy-start | bytes 393220
  17.7 411.2 %all-gather.3.cloned.1.call-start = ((), (), s32[]{:S(2)}) async-start(), calls=%async_computation.4 | async-start | bytes 4259840 | tf_op jit(solution)/shard_map/all_gather | solution.py:22
  320.3 112.8 %all-to-all-start = ((bf16[64,2,256]{2,1,0:T(2,128)(2,1)}), bf16[64,2,256]{2,1,0:T(2,128)(2,1)S(1)}, u32[]{:S(2)}, u32[]{:S(2)}) async-start(bf16[64,2,256]{2,1,0:T(2,128)(2,1)} %reshape.10), calls=%async_computation.1 | async-start | bytes 131072 | tf_op jit(solution)/shard_map/all_to_all | solution.py:27
  330.6 148.4 %all-reduce.2.cloned.1.call-start = ((), (), s32[]{:S(2)}) async-start(), calls=%async_computation.5 | async-start | bytes 131072 | tf_op jit(solution)/shard_map/psum | solution.py:25
  433.0 157.9 %all-gather.5.cloned.1.call-start = ((), (), s32[]{:S(2)}) async-start(), calls=%async_computation.6 | async-start | bytes 4259840 | tf_op jit(solution)/shard_map/all_gather | solution.py:31
  434.1 453.5 %reduce-scatter.5.cloned.1.call-start = ((), (), s32[]{:S(2)}) async-start(), calls=%async_computation.7 | async-start | bytes 8519680 | tf_op jit(solution)/shard_map/reduce_scatter | solution.py:36
  438.6 40.4 %copy-start.3 = (f32[16,1024]{1,0:T(8,128)S(1)}, f32[16,1024]{1,0:T(8,128)}, u32[]{:S(2)}) copy-start(f32[16,1024]{1,0:T(8,128)} %param.7) | copy-start | bytes 196612
  438.6 152.3 %copy-start.1 = (f32[1,32,2048]{2,1,0:T(8,128)S(1)}, f32[1,32,2048]{2,1,0:T(8,128)}, u32[]{:S(2)}) copy-start(f32[1,32,2048]{2,1,0:T(8,128)} %param.8) | copy-start | bytes 786436
Sparse Core Ops, SparseCore 0:
  17.9 298.7 reduce-scatter.2
  319.1 109.7 all-gather.2
  433.1 45.7 all-reduce.1
  481.4 109.4 all-gather.4
  593.4 294.0 reduce-scatter.4
where the time goes:
time: 900 us; the launch traced here: 896 us
  waiting for transfers between devices  840 us (93%)
  matrix products  21.7 us (2%)
  between operations  13.8 us (2%)
  starting transfers between devices  10.5 us (1%)
    reduce_scatter x1, waiting for transfers between devices, body(): lax.psum_scatter(jnp.einsum('tr,tc->rc', attn_out, out_grad, preferred_el...  299 us
    reduce_scatter x1, waiting for transfers between devices, body(): lax.psum_scatter(jnp.dot(columns, basis_rows, preferred_element_type=jnp....  292 us
    all_gather x1, waiting for transfers between devices, body(): lax.all_gather(columns, 'dp', axis=1, tiled=True)  110 us
    all_gather x1, waiting for transfers between devices, body(): lax.all_gather(grad_b, 'dp', axis=0, tiled=True)  98.3 us
    psum x1, waiting for transfers between devices, body(): total = lax.psum(partial_gram, 'mp')  40.4 us
  transfers between devices with their start and end apart: 6, of which 5 were waited for; matrix products, arithmetic and copies ran while one was open for 2% of the time, Pallas kernels for 0%

commit v1 on v0

v1 whole, which is shorter than its diff:
```python
import functools

import jax
import jax.numpy as jnp
from jax import lax
from jax.experimental import pallas as pl
from jax.experimental.pallas import tpu as pltpu
from jax.sharding import PartitionSpec as P

MESH = pl.DeviceIdType.MESH
F32 = jnp.float32
BF16 = jnp.bfloat16

ROWS = 1024
TOK = 1024
COLS = 2048
HALF = 1024
W = 256
NC = HALF // W
N_SEM = 48 * NC + 48


def rows(start, size, unit=16):
    return pl.ds(pl.multiple_of(start, unit), size)


def kernel(
    a_hbm, g_hbm, left_hbm, right_hbm, basis_hbm,
    left_out, right_out, rot_out,
    a_v, at_v, g_v, p_v, pr_v, o_v, r1_v, t1_v, r2_v, t2_v, r3_v, cf_v,
    basis_v, bp_v, left_v, right_v, lacc_v, lr_v, ltot_v, racc_v, rsend_v, ct_v,
    ssem, rsem, lsem,
):
    dp = lax.axis_index("dp")
    mp = lax.axis_index("mp")
    x, z, y, c = dp // 16, (dp // 8) % 2, (dp // 2) % 4, dp % 2
    i1 = x * (1 - c) + y * c
    i2 = y * (1 - c) + x * c
    s1 = 16 * (1 - c) + 2 * c
    s2 = 2 * (1 - c) + 16 * c
    right1 = dp + ((i1 + 1) % 4 - i1) * s1
    left1 = dp + ((i1 + 3) % 4 - i1) * s1
    right2 = dp + ((i2 + 1) % 4 - i2) * s2
    left2 = dp + ((i2 + 3) % 4 - i2) * s2
    other_core = dp + 1 - 2 * c
    other_z = dp + (1 - 2 * z) * 8

    def plane(dx, dy):
        return ((x + dx) % 4) * 16 + z * 8 + ((y + dy) % 4) * 2 + c

    loads = {}

    def load(name, src, dst):
        copy = pltpu.make_async_copy(src, dst, lsem.at[len(loads)])
        copy.start()
        loads[name] = copy

    def a_load(r):
        load(("a", r), a_hbm.at[:, pl.ds(256 * r, 256)], a_v.at[r])

    def g_load(own, j):
        half = c if own else 1 - c
        load(
            ("g", own, j),
            g_hbm.at[:, pl.ds(pl.multiple_of(half * HALF + j * W, W), W)],
            g_v.at[j if own else NC + j],
        )

    a_load(0)
    g_load(False, 0)
    for r in range(1, 4):
        a_load(r)
    load("basis", basis_hbm.at[0], basis_v)
    g_load(True, 0)
    for j in range(1, NC):
        g_load(False, j)
        g_load(True, j)
    load("left", left_hbm, left_v)
    load("right", right_hbm.at[0], right_v)

    barrier = pltpu.get_barrier_semaphore()
    offsets = [(dx, dy) for dx in range(4) for dy in range(4) if (dx, dy) != (0, 0)]
    for dx, dy in offsets:
        pl.semaphore_signal(barrier, inc=1, device_id=(plane(dx, dy), mp), device_id_type=MESH)
    for device in (other_core, other_z):
        pl.semaphore_signal(barrier, inc=1, device_id=(device, mp), device_id_type=MESH)
    for d in range(1, 4):
        pl.semaphore_signal(barrier, inc=1, device_id=(dp, (mp + d) % 4), device_id_type=MESH)

    slots = {}
    started = []

    def slot(name):
        return slots.setdefault(name, len(slots))

    def send(name, src, dst, device, mp_to=None):
        n = slot(name)
        copy = pltpu.make_async_remote_copy(
            src_ref=src, dst_ref=dst, send_sem=ssem.at[n], recv_sem=rsem.at[n],
            device_id=(device, mp if mp_to is None else mp_to), device_id_type=MESH,
        )
        copy.start()
        started.append(copy)

    def recv(name, dst):
        n = slot(name)
        pltpu.make_async_remote_copy(
            src_ref=dst, dst_ref=dst, send_sem=ssem.at[n], recv_sem=rsem.at[n],
            device_id=(other_core, mp), device_id_type=MESH,
        ).wait_recv()

    def drain(count):
        for _ in range(min(count, len(started))):
            started.pop(0).wait_send()

    for r in range(4):
        loads[("a", r)].wait()
        at_v[256 * r:256 * (r + 1), :] = a_v[r].T

    pl.semaphore_wait(barrier, len(offsets) + 5)

    loads["basis"].wait()
    p_me = 4 * x + y
    zc = 2 * z + c

    def basis_slot(g, p):
        return bp_v.at[g, rows(p * 32, 32)]

    for dx, dy in offsets:
        p_to = 4 * ((x + dx) % 4) + (y + dy) % 4
        send(("basis", dx, dy), basis_v.at[:, rows(p_to * 128, 128, 128)], basis_slot(zc, p_me), plane(dx, dy))
    bp_v[zc, rows(p_me * 32, 32)] = basis_v[:, rows(p_me * 128, 128, 128)]

    def basis_gather():
        for dx, dy in offsets:
            p_from = 4 * ((x - dx + 4) % 4) + (y - dy + 4) % 4
            recv(("basis", dx, dy), basis_slot(zc, p_from))
        send("basis_core", bp_v.at[zc], bp_v.at[zc], other_core)
        send("basis_z", bp_v.at[zc], bp_v.at[zc], other_z)

    def basis_forward():
        from_z = 2 * (1 - z) + c
        recv("basis_z", bp_v.at[from_z])
        send("basis_fwd", bp_v.at[from_z], bp_v.at[from_z], other_core)

    def basis_end():
        recv("basis_core", bp_v.at[2 * z + 1 - c])
        recv("basis_fwd", bp_v.at[2 * (1 - z) + 1 - c])

    def compute(j):
        base = len(slots)
        for t in range(4):
            slot(("pair", j, t))
        loads[("g", False, j)].wait()

        def partner(t, carry):
            block = rows(((i2 + 6 - t) % 4) * 256, 256)
            p_v[j, block] = jnp.dot(at_v[block, :], g_v[NC + j], preferred_element_type=F32)
            pltpu.make_async_remote_copy(
                src_ref=p_v.at[j, block], dst_ref=pr_v.at[j, block],
                send_sem=ssem.at[base + t], recv_sem=rsem.at[base + t],
                device_id=(other_core, mp), device_id_type=MESH,
            ).start()
            return carry

        lax.fori_loop(0, 4, partner, 0)
        for t in range(4):
            block = rows(((i2 + 6 - t) % 4) * 256, 256)
            started.append(pltpu.make_async_remote_copy(
                src_ref=p_v.at[j, block], dst_ref=pr_v.at[j, block],
                send_sem=ssem.at[base + t], recv_sem=rsem.at[base + t],
                device_id=(other_core, mp), device_id_type=MESH,
            ))
        loads[("g", True, j)].wait()

        def own(t, carry):
            block = rows(((i1 + 6 - t) % 4) * 256, 256)
            o_v[j, block] = jnp.dot(at_v[block, :], g_v[j], preferred_element_type=F32)
            return carry

        lax.fori_loop(0, 4, own, 0)

    def pair_add(j, t):
        block = rows(((i1 + 6 - t) % 4) * 256, 256)
        recv(("pair", j, t), pr_v.at[j, block])
        o_v[j, block] += pr_v[j, block]

    def ring(tag, src, land, unit, i, to_right, to_left):
        h = unit // 2

        def part(q, half):
            return rows((q % 4) * unit + half * h, h)

        def far():
            send((tag, 0), src.at[part(i + 2, 0)], land.at[0], to_right)
            send((tag, 1), src.at[part(i + 2, 1)], land.at[1], to_left)

        def direct_right():
            send((tag, 2), src.at[part(i + 1, 1)], land.at[2], to_right)

        def direct_left():
            send((tag, 3), src.at[part(i + 3, 0)], land.at[3], to_left)

        def aggregate():
            recv((tag, 0), land.at[0])
            src[part(i + 1, 0), :] += land[0]
            send((tag, 4), src.at[part(i + 1, 0)], land.at[4], to_right)
            recv((tag, 1), land.at[1])
            src[part(i + 3, 1), :] += land[1]
            send((tag, 5), src.at[part(i + 3, 1)], land.at[5], to_left)

        def finish(dst):
            recv((tag, 2), land.at[2])
            recv((tag, 3), land.at[3])
            recv((tag, 4), land.at[4])
            dst[0:h, :] = src[part(i, 0), :] + land[3] + land[4]
            recv((tag, 5), land.at[5])
            dst[h:unit, :] = src[part(i, 1), :] + land[2] + land[5]

        return far, direct_right, direct_left, aggregate, finish

    def gather(tag, buf, base, unit, i, to_right, to_left):
        h = unit // 2

        def part(q, half, size):
            return rows(base + (q % 4) * unit + half * h, size)

        def begin():
            own = buf.at[part(i, 0, unit)]
            send((tag, 0), own, own, to_right)
            send((tag, 1), own, own, to_left)

        def forward():
            recv((tag, 0), buf.at[part(i + 3, 0, unit)])
            half = buf.at[part(i + 3, 0, h)]
            send((tag, 2), half, half, to_right)
            recv((tag, 1), buf.at[part(i + 1, 0, unit)])
            half = buf.at[part(i + 1, 1, h)]
            send((tag, 3), half, half, to_left)

        def end():
            recv((tag, 2), buf.at[part(i + 2, 0, h)])
            recv((tag, 3), buf.at[part(i + 2, 1, h)])

        return begin, forward, end

    lacc_v[...] = jnp.zeros_like(lacc_v)
    racc_v[...] = jnp.zeros_like(racc_v)

    def chunk(j):
        k = NC * c + j
        k_other = NC * (1 - c) + j
        buf = cf_v.at[k]
        ring1 = ring(("r1", j), o_v.at[j], r1_v.at[j], 256, i1, right1, left1)
        ring2 = ring(("r2", j), t1_v.at[j], r2_v.at[j], 64, i2, right2, left2)
        gather2 = gather(("g2", j), buf, i1 * 256, 64, i2, right2, left2)
        gather1 = gather(("g1", j), buf, 0, 256, i1, right1, left1)
        row0 = i1 * 256 + i2 * 64

        def to_core(q, n):
            block = buf.at[rows((q % 4) * 256, 256)]
            send(("core", j, n), block, block, other_core)

        def act0():
            compute(j)

        def act1():
            pair_add(j, 0)
            ring1[0]()
            pair_add(j, 1)
            ring1[1]()
            pair_add(j, 3)
            ring1[2]()
            pair_add(j, 2)

        def act2():
            ring1[3]()

        def act3():
            ring1[4](t1_v.at[j])
            ring2[0]()
            ring2[1]()
            ring2[2]()

        def act4():
            ring2[3]()

        def act5():
            ring2[4](t2_v.at[j])
            send(("z", j), t2_v.at[j, rows((1 - z) * 32, 32)], r3_v.at[j], other_z)

        def act6():
            recv(("z", j), r3_v.at[j])
            mine = buf.at[rows(row0 + z * 32, 32)]
            mine[...] = (t2_v[j, rows(z * 32, 32)] + r3_v[j]).astype(BF16)
            send(("gz", j), mine, mine, other_z)

        def act7():
            recv(("gz", j), buf.at[rows(row0 + (1 - z) * 32, 32)])
            gather2[0]()

        def act8():
            gather2[1]()

        def act9():
            gather2[2]()
            gather1[0]()
            to_core(i1, 0)

        def act10():
            gather1[1]()
            to_core(i1 + 3, 1)
            to_core(i1 + 1, 2)

        def act11():
            gather1[2]()
            to_core(i1 + 2, 3)

        def act12():
            other = cf_v.at[k_other]
            for n, q in enumerate((i2, i2 + 3, i2 + 1, i2 + 2)):
                recv(("core", j, n), other.at[rows((q % 4) * 256, 256)])

        def act13():
            def one(n, carry):
                kk = NC * n + j
                lacc_v[...] += lax.dot_general(
                    cf_v[kk, rows(dp * 16, 16)], cf_v[kk], (((1,), (1,)), ((), ())),
                    preferred_element_type=F32,
                )
                lhs = jnp.concatenate(
                    [cf_v[kk, rows(256 * xx + 128 * z + 32 * yy + 16 * c, 16)] for xx in range(4) for yy in range(4)], 0
                )
                rhs = jnp.concatenate(
                    [bp_v[2 * (kk % 2) + cc, rows((4 * (kk // 2) + yy) * 32, 32)] for yy in range(4) for cc in range(2)], 0
                )
                racc_v[...] += jnp.dot(lhs, rhs, preferred_element_type=F32)
                return carry

            lax.fori_loop(0, 2, one, 0)

        return (act0, act1, act2, act3, act4, act5, act6, act7, act8, act9, act10, act11, act12, act13)

    chunks = [chunk(j) for j in range(NC)]
    period, start = 4.0, (0.0, 1.5, 3.5, 6.0, 7.5, 9.0, 10.5, 12.0, 13.5, 15.0, 17.0, 19.0, 20.5, 21.0)
    order = sorted((j * period + start[s], s, j) for j in range(NC) for s in range(len(start)))
    marks = {(0, 1): basis_gather, (0, 2): basis_forward, (0, 5): basis_end}
    for _, s, j in order:
        if (j, s) in marks:
            marks[(j, s)]()
        chunks[j][s]()
        if s >= 7:
            drain(8)

    def quarter(ref, m):
        return ref.at[:, rows((m % 4) * 256, 256, 256)]

    for d in range(1, 4):
        send(("ls", d), quarter(lacc_v, mp + d), lr_v.at[d], dp, (mp + d) % 4)

    rsend_v[...] = racc_v[...].astype(BF16)
    mine = rows(p_me * 128, 128, 128)
    for dx, dy in offsets:
        p_to = 4 * ((x + dx) % 4) + (y + dy) % 4
        send(("rot", dx, dy), rsend_v.at[rows(p_to * 16, 16)], rot_out.at[:, mine], plane(dx, dy))
    rot_out[:, mine] = rsend_v[rows(p_me * 16, 16), :]

    group = rows(128 * ((dp // 4) % 2), 128, 128)
    ct_v[...] = cf_v[dp // 8, :, group].T
    loads["right"].wait()

    def right_step(k, carry):
        cols = rows(k * 256, 256, 256)
        gram = jnp.dot(ct_v[rows(32 * (dp % 4), 32), :], cf_v[k], preferred_element_type=F32)
        right_out[0, :, cols] = 0.9 * right_v[:, cols] + 0.1 * (gram / ROWS)
        return carry

    lax.fori_loop(0, 4, right_step, 0)

    for d in range(1, 4):
        recv(("ls", d), lr_v.at[d])
    my_quarter = rows(mp * 256, 256, 256)
    ltot_v[:, my_quarter] = lacc_v[:, my_quarter] + lr_v[1] + lr_v[2] + lr_v[3]
    for d in range(1, 4):
        send(("lg", d), quarter(ltot_v, mp), quarter(ltot_v, mp), dp, (mp + d) % 4)

    lax.fori_loop(4, 8, right_step, 0)

    loads["left"].wait()
    for d in range(1, 4):
        recv(("lg", d), quarter(ltot_v, mp + 4 - d))
    left_out[...] = 0.9 * left_v[...] + 0.1 * (ltot_v[...] / (4 * COLS))
    for dx, dy in offsets:
        p_from = 4 * ((x - dx + 4) % 4) + (y - dy + 4) % 4
        recv(("rot", dx, dy), rot_out.at[:, rows(p_from * 128, 128, 128)])
    drain(len(started))


def body(attn_out, out_grad, left_old, right_old, basis):
    vmem = pl.BlockSpec(memory_space=pltpu.VMEM)
    hbm = pl.BlockSpec(memory_space=pl.ANY)
    v = pltpu.VMEM
    return pl.pallas_call(
        kernel,
        out_shape=(
            jax.ShapeDtypeStruct((16, ROWS), F32),
            jax.ShapeDtypeStruct((1, 32, COLS), F32),
            jax.ShapeDtypeStruct((16, COLS), BF16),
        ),
        in_specs=[hbm] * 5,
        out_specs=(vmem, vmem, vmem),
        scratch_shapes=[
            v((4, TOK, 256), BF16),
            v((ROWS, TOK), BF16),
            v((2 * NC, TOK, W), BF16),
            v((NC, ROWS, W), F32),
            v((NC, ROWS, W), F32),
            v((NC, ROWS, W), F32),
            v((NC, 6, 128, W), F32),
            v((NC, 256, W), F32),
            v((NC, 6, 32, W), F32),
            v((NC, 64, W), F32),
            v((NC, 32, W), F32),
            v((2 * NC, ROWS, W), BF16),
            v((32, COLS), BF16),
            v((4, 512, 128), BF16),
            v((16, ROWS), F32),
            v((32, COLS), F32),
            v((16, ROWS), F32),
            v((4, 16, 256), F32),
            v((16, ROWS), F32),
            v((256, 128), F32),
            v((256, 128), BF16),
            v((128, ROWS), BF16),
            pltpu.SemaphoreType.DMA((N_SEM,)),
            pltpu.SemaphoreType.DMA((N_SEM,)),
            pltpu.SemaphoreType.DMA((8 + 2 * NC,)),
        ],
        compiler_params=pltpu.CompilerParams(
            collective_id=0, has_side_effects=True, vmem_limit_bytes=52 * 1024 * 1024,
        ),
        cost_estimate=pl.CostEstimate(flops=5 * 10**9, bytes_accessed=7 * 2**20, transcendentals=0),
    )(attn_out, out_grad, left_old, right_old, basis)


def solution(mesh):
    return jax.shard_map(
        body,
        mesh=mesh,
        in_specs=(
            P("dp", None),
            P("dp", "mp"),
            P("dp", None),
            P("mp", "dp", None),
            P("mp", "dp", None),
        ),
        out_specs=(P("dp", None), P("mp", "dp", None), P("dp", "mp")),
        check_vma=False,
    )
```

time: 900 us -> 102 us (0.11)
  waiting for transfers between devices: 840 us -> 0 us
  Pallas kernels: 0 us -> 96.3 us
  matrix products: 21.7 us -> 0 us
  between operations: 13.8 us -> 0.65 us
  starting transfers between devices: 10.5 us -> 0 us
    reduce_scatter x2 -> x0, waiting for transfers between devices: 591 us -> none  [the longest x1 299 us: body(): lax.psum_scatter(jnp.einsum('tr,tc->rc', attn_out, out_grad, preferred_el...]
    all_gather x2 -> x0, waiting for transfers between devices: 209 us -> none  [the longest x1 110 us: body(): lax.all_gather(columns, 'dp', axis=1, tiled=True)]
    pallas_call x0 -> x1, Pallas kernels: none -> 96.3 us  [body(): pl.pallas_call(kernel, out_shape=(jax.ShapeDtypeStruct((16, ROWS), F32),...]
    psum x1 -> x0, waiting for transfers between devices: 40.4 us -> none  [body(): total = lax.psum(partial_gram, 'mp')]
    dot_general x4 -> x0, matrix products: 21.7 us -> none  [the longest x1 8.94 us: body(): jnp.einsum('tr,tc->rc', attn_out, out_grad, preferred_element_type=jnp.fl...]
    all_to_all x1 -> x0, starting transfers between devices: 10.3 us -> none  [body(): lax.all_to_all(grad_b, 'dp', split_axis=1, concat_axis=0, tiled=True)]
  transfers between devices with their start and end apart: 6 -> 0, of which waited for: 5 -> 0; matrix products, arithmetic and copies ran while one was open for 2% -> 0% of each run, Pallas kernels for 0% -> 0%
where the time goes in v1:
time: 102 us
  Pallas kernels  96.3 us (94%)
  local copies, waits for them, and re-layouts  4.65 us (5%)
    pallas_call x1, Pallas kernels, body(): pl.pallas_call(kernel, out_shape=(jax.ShapeDtypeStruct((16, ROWS), F32),...  96.3 us
    unnamed x9, local copies, waits for them, and re-layouts  4.65 us

profile of v1, /device:TPU:1, one launch (start us, length us, event | category | flops | bytes accessed | tf_op | source)
XLA Modules:
  0.0 101.6 jit_solution(9276525147394671482)
XLA Ops:
  0.6 0.0 copy-start
  0.6 0.9 copy-done
  1.6 0.0 copy-start.1
  1.6 0.9 copy-done.1
  2.5 0.0 copy-start.2
  2.5 0.8 copy-done.2
  3.3 96.3 %shard_map.76 = (f32[16,1024]{1,0:T(8,128)S(1)}, f32[1,32,2048]{2,1,0:T(8,128)S(1)}, bf16[16,2048]{1,0:T(8,128)(2,1)S(1)}) custom-call(bf16[1024,1024]{1,0:T(8,128)(2,1)} %a_hbm.1, bf16[1024,2048]{1,0:T(8,128)(2,1)} %g_hbm.1, f32[16,1024]{1,0:T(8,128)S(1)} %copy-done.2, f32[1,32,2048]{2,1,0:T(8,128)S(1)} %copy-done, bf16[1,32,2048]{2,1,0:T(8,128)(2,1)S(1)} %copy-done.1), custom_call_target="tpu_custom_call" | custom-call | flops 5000000000 | bytes 7340032 | tf_op jit(solution)/shard_map/pallas_call | solution.py:403
  99.6 0.6 copy.11
  100.2 0.7 copy.12
  100.9 0.6 copy.13
Async XLA Ops:
  0.6 1.0 copy-start
  1.6 0.9 copy-start.1
  2.5 0.8 copy-start.2

commit v2 on v0

v2 whole, which is shorter than its diff:
```python
import jax
import jax.numpy as jnp
from jax import lax
from jax.experimental import pallas as pl
from jax.experimental.pallas import tpu as pltpu
from jax.sharding import PartitionSpec as P

MESH = pl.DeviceIdType.MESH
F32 = jnp.float32
BF16 = jnp.bfloat16

ROWS = 1024
TOK = 1024
COLS = 2048
HALF = 1024
W = 256
NC = HALF // W

PLANE = [(dx, dy) for dx in range(4) for dy in range(4) if (dx, dy) != (0, 0)]
EIGHT = [(di, dz) for di in range(4) for dz in range(2) if (di, dz) != (0, 0)]

ORDER = [
    ("partner", 1), ("own", 0), ("partner", 2), ("own", 1), ("far", 0), ("partner", 3), ("own", 2),
    ("direct", 0), ("far", 1), ("own", 3), ("aggregate", 0), ("direct", 1), ("far", 2), ("direct", 2),
    ("far", 3), ("aggregate", 1), ("direct", 3), ("finish", 0), ("aggregate", 2), ("aggregate", 3),
    ("finish", 1), ("total", 0), ("basis_gather", 0), ("finish", 2), ("finish", 3), ("total", 1), ("gather", 0),
    ("total", 2), ("total", 3), ("basis_forward", 0), ("forward", 0), ("gather", 1), ("gather", 2), ("end", 0),
    ("gather", 3), ("basis_end", 0), ("products", 0), ("forward", 1), ("forward", 2), ("forward", 3), ("end", 1),
    ("end", 2), ("products", 1), ("end", 3), ("products", 2), ("products", 3),
]


def rows(start, size, unit=16):
    return pl.ds(pl.multiple_of(start, unit), size)


def kernel(
    a_hbm, g_hbm, left_hbm, right_hbm, basis_hbm,
    left_out, right_out, rot_out,
    a_v, g_v, p_v, pr_v, o_v, r1_v, t1_v, r2_v, cf_v,
    basis_v, bp_v, left_v, right_v, lacc_v, lr_v, racc_v, rsend_v, ct_v,
    ssem, rsem, lsem,
):
    dp = lax.axis_index("dp")
    mp = lax.axis_index("mp")
    x, z, y, c = dp // 16, (dp // 8) % 2, (dp // 2) % 4, dp % 2
    i1 = x * (1 - c) + y * c
    i2 = y * (1 - c) + x * c
    s1 = 16 * (1 - c) + 2 * c
    s2 = 2 * (1 - c) + 16 * c
    right1 = dp + ((i1 + 1) % 4 - i1) * s1
    left1 = dp + ((i1 + 3) % 4 - i1) * s1
    other_core = dp + 1 - 2 * c
    other_z = dp + (1 - 2 * z) * 8

    def plane(dx, dy):
        return ((x + dx) % 4) * 16 + z * 8 + ((y + dy) % 4) * 2 + c

    def eight(di, dz):
        return dp + ((i2 + di) % 4 - i2) * s2 + ((z + dz) % 2 - z) * 8

    barrier = pltpu.get_barrier_semaphore()
    greeted = [(plane(dx, dy), mp) for dx, dy in PLANE] + [(eight(di, 1), mp) for di in range(4)]
    greeted += [(other_core, mp)] + [(dp, (mp + d) % 4) for d in range(1, 4)]
    for device in greeted:
        pl.semaphore_signal(barrier, inc=1, device_id=device, device_id_type=MESH)

    loads = {}

    def load(name, src, dst):
        copy = pltpu.make_async_copy(src, dst, lsem.at[len(loads)])
        copy.start()
        loads[name] = copy

    def g_load(own, j):
        half = c if own else 1 - c
        load(
            ("g", own, j),
            g_hbm.at[:, rows(half * HALF + j * W, W, W)],
            g_v.at[j if own else NC + j],
        )

    load("a", a_hbm, a_v)
    g_load(False, 0)
    g_load(True, 0)
    load("basis", basis_hbm.at[0], basis_v)
    for j in range(1, NC):
        g_load(False, j)
        g_load(True, j)
    load("left", left_hbm, left_v)
    load("right", right_hbm.at[0], right_v)

    sent, landed = {}, {}

    def descriptor(src, dst, out, into, device):
        return pltpu.make_async_remote_copy(
            src_ref=src, dst_ref=dst,
            send_sem=ssem.at[sent.setdefault(out, len(sent))],
            recv_sem=rsem.at[landed.setdefault(into, len(landed))],
            device_id=device, device_id_type=MESH,
        )

    def send(src, dst, out, into, device):
        descriptor(src, dst, out, into, device).start()

    def recv(into, span):
        pltpu.make_async_copy(span, span, rsem.at[landed[into]]).wait()

    def wait_sent(out, span):
        pltpu.make_async_copy(span, span, ssem.at[sent[out]]).wait()

    p_me = 4 * x + y
    zc = 2 * z + c

    def basis_begin():
        loads["basis"].wait()
        for dx, dy in PLANE:
            p_to = 4 * ((x + dx) % 4) + (y + dy) % 4
            send(
                basis_v.at[:, rows(p_to * 128, 128, 128)], bp_v.at[zc, rows(p_me * 32, 32)],
                "basis", "basis", (plane(dx, dy), mp),
            )
        bp_v[zc, rows(p_me * 32, 32)] = basis_v[:, rows(p_me * 128, 128, 128)]

    def basis_gather():
        recv("basis", bp_v.at[zc, 0:480])
        send(bp_v.at[zc], bp_v.at[zc], "basis_core", "basis_core", (other_core, mp))
        send(bp_v.at[zc], bp_v.at[zc], "basis_z", "basis_z", (other_z, mp))

    def basis_forward():
        from_z = 2 * (1 - z) + c
        recv("basis_z", bp_v.at[from_z])
        send(bp_v.at[from_z], bp_v.at[from_z], "basis_forward", "basis_forward", (other_core, mp))

    def basis_end():
        recv("basis_core", bp_v.at[2 * z + 1 - c])
        recv("basis_forward", bp_v.at[2 * (1 - z) + 1 - c])

    def quarter1(i):
        return (i % 4) * 256

    def partner_product(j):
        loads[("g", False, j)].wait()
        p_v[j] = lax.dot_general(a_v[...], g_v[NC + j], (((0,), (0,)), ((), ())), preferred_element_type=F32)

    def partner_send(j):
        if j == 0:
            for t in (2, 1, 3, 0):
                block = rows(quarter1(i2 + t), 256)
                send(p_v.at[j, block], pr_v.at[j, block], "pair", ("pair", j, t), (other_core, mp))
        else:
            send(p_v.at[j], pr_v.at[j], "pair", ("pair", j), (other_core, mp))

    def partner(j):
        partner_product(j)
        partner_send(j)

    def own(j):
        loads[("g", True, j)].wait()
        o_v[j] = lax.dot_general(a_v[...], g_v[j], (((0,), (0,)), ((), ())), preferred_element_type=F32)

    def part(i, half):
        return rows(quarter1(i) + half * 128, 128)

    def far(j):
        for t in (2, 1, 3, 0):
            block = rows(quarter1(i1 + t), 256)
            if j == 0:
                recv(("pair", j, t), pr_v.at[j, block])
            elif t == 2:
                recv(("pair", j), pr_v.at[j])
            o_v[j, block] += pr_v[j, block]
            if t == 2:
                src, land = o_v.at[j], r1_v.at[j]
                send(src.at[part(i1 + 2, 0)], land.at[0], "ring", ("far", j), (right1, mp))
                send(src.at[part(i1 + 2, 1)], land.at[1], "ring", ("far", j), (left1, mp))

    def direct(j):
        src, land = o_v.at[j], r1_v.at[j]
        send(src.at[part(i1 + 1, 1)], land.at[2], "ring", ("near", j), (right1, mp))
        send(src.at[part(i1 + 3, 0)], land.at[3], "ring", ("near", j), (left1, mp))

    def aggregate(j):
        src, land = o_v.at[j], r1_v.at[j]
        recv(("far", j), land.at[0:2])
        src[part(i1 + 1, 0), :] += land[0]
        send(src.at[part(i1 + 1, 0)], land.at[4], "ring", ("near", j), (right1, mp))
        src[part(i1 + 3, 1), :] += land[1]
        send(src.at[part(i1 + 3, 1)], land.at[5], "ring", ("near", j), (left1, mp))

    def finish(j):
        src, land, dst = o_v.at[j], r1_v.at[j], t1_v.at[j]
        recv(("near", j), land.at[2:6])
        dst[0:128, :] = src[part(i1, 0), :] + land[3] + land[4]
        dst[128:256, :] = src[part(i1, 1), :] + land[2] + land[5]
        for n, (di, dz) in enumerate(EIGHT):
            block = rows(((i2 + di) % 4) * 64 + ((z + dz) % 2) * 32, 32)
            send(dst.at[block], r2_v.at[j, n], "eight", ("eight", j), (eight(di, dz), mp))

    def total(j):
        recv(("eight", j), r2_v.at[j])
        value = t1_v[j, rows(i2 * 64 + z * 32, 32)]
        for n in range(len(EIGHT)):
            value += r2_v[j, n]
        mine = cf_v.at[NC * c + j, rows(i1 * 256 + i2 * 64 + z * 32, 32)]
        mine[...] = value.astype(BF16)
        for di, dz in EIGHT:
            send(mine, mine, ("all8", j), ("all8", j), (eight(di, dz), mp))

    def to_core(j, i):
        block = cf_v.at[NC * c + j, rows(quarter1(i), 256)]
        send(block, block, ("core", j), ("core", j), (other_core, mp))

    def gather(j):
        buf = cf_v.at[NC * c + j]
        recv(("all8", j), buf.at[rows(quarter1(i1), 224)])
        block = buf.at[rows(quarter1(i1), 256)]
        send(block, block, ("ring8", j), ("begin", j), (right1, mp))
        send(block, block, ("ring8", j), ("begin", j), (left1, mp))
        to_core(j, i1)

    def forward(j):
        buf = cf_v.at[NC * c + j]
        recv(("begin", j), buf.at[0:512])
        half = buf.at[part(i1 + 3, 0)]
        send(half, half, ("ring8", j), ("forward", j), (right1, mp))
        half = buf.at[part(i1 + 1, 1)]
        send(half, half, ("ring8", j), ("forward", j), (left1, mp))
        to_core(j, i1 + 3)
        to_core(j, i1 + 1)

    def end(j):
        recv(("forward", j), cf_v.at[NC * c + j, 0:256])
        to_core(j, i1 + 2)

    def products(j):
        recv(("core", j), cf_v.at[NC * (1 - c) + j])

        def one(n, carry):
            k = NC * n + j
            lacc_v[...] += lax.dot_general(
                cf_v[k, rows(dp * 16, 16)], cf_v[k], (((1,), (1,)), ((), ())), preferred_element_type=F32
            )
            lhs = jnp.concatenate(
                [cf_v[k, rows(256 * xx + 128 * z + 32 * yy + 16 * c, 16)] for xx in range(4) for yy in range(4)], 0
            )
            rhs = jnp.concatenate(
                [bp_v[2 * (k % 2) + cc, rows((4 * (k // 2) + yy) * 32, 32)] for yy in range(4) for cc in range(2)], 0
            )
            racc_v[...] += jnp.dot(lhs, rhs, preferred_element_type=F32)
            return carry

        lax.fori_loop(0, 2, one, 0)

    steps = {
        "partner": partner, "own": own, "far": far, "direct": direct, "aggregate": aggregate, "finish": finish,
        "total": total, "gather": gather, "forward": forward, "end": end, "products": products,
        "basis_gather": lambda j: basis_gather(), "basis_forward": lambda j: basis_forward(),
        "basis_end": lambda j: basis_end(),
    }

    loads["a"].wait()
    with jax.named_scope("first"):
        partner_product(0)
        lacc_v[...] = jnp.zeros_like(lacc_v)
        racc_v[...] = jnp.zeros_like(racc_v)
    with jax.named_scope("barrier"):
        pl.semaphore_wait(barrier, len(greeted))
    partner_send(0)
    basis_begin()
    for step, j in ORDER:
        with jax.named_scope(f"{step}_{j}"):
            steps[step](j)

    with jax.named_scope("left_send"):
        lr_v[mp] = lacc_v[...].astype(BF16)
        for d in range(1, 4):
            send(lr_v.at[mp], lr_v.at[mp], "left", "left", (dp, (mp + d) % 4))

    with jax.named_scope("rotated_send"):
        rsend_v[...] = racc_v[...].astype(BF16)
        mine = rows(p_me * 128, 128, 128)
        for dx, dy in PLANE:
            p_to = 4 * ((x + dx) % 4) + (y + dy) % 4
            send(rsend_v.at[rows(p_to * 16, 16)], rot_out.at[:, mine], "rotated", "rotated", (plane(dx, dy), mp))
        rot_out[:, mine] = rsend_v[rows(p_me * 16, 16), :]

    with jax.named_scope("right"):
        ct_v[...] = cf_v[dp // 8, :, rows(128 * ((dp // 4) % 2), 128, 128)].T
        loads["right"].wait()

        def right_step(k, carry):
            cols = rows(k * 256, 256, 256)
            gram = jnp.dot(ct_v[rows(32 * (dp % 4), 32), :], cf_v[k], preferred_element_type=F32)
            right_out[0, :, cols] = 0.9 * right_v[:, cols] + 0.1 * (gram / ROWS)
            return carry

        lax.fori_loop(0, 2 * NC, right_step, 0)

    with jax.named_scope("sent"):
        wait_sent("pair", p_v)
        wait_sent("ring", r1_v)
        wait_sent("eight", r2_v)
        for j in range(NC):
            wait_sent(("all8", j), cf_v.at[0, 0:224])
            wait_sent(("ring8", j), cf_v.at[0, 0:768])
            wait_sent(("core", j), cf_v.at[0])
        wait_sent("basis", bp_v.at[0, 0:480])
        for name in ("basis_core", "basis_z", "basis_forward"):
            wait_sent(name, bp_v.at[0])
        wait_sent("rotated", rsend_v.at[0:240])
        wait_sent("left", lr_v.at[0:3])
    with jax.named_scope("rotated_recv"):
        recv("rotated", rsend_v.at[0:240])
    with jax.named_scope("left_recv"):
        loads["left"].wait()
        recv("left", lr_v.at[0:3])
        gram = lr_v[0].astype(F32) + lr_v[1].astype(F32) + lr_v[2].astype(F32) + lr_v[3].astype(F32)
        left_out[...] = 0.9 * left_v[...] + 0.1 * (gram / (4 * COLS))


def body(attn_out, out_grad, left_old, right_old, basis):
    vmem = pl.BlockSpec(memory_space=pltpu.VMEM)
    hbm = pl.BlockSpec(memory_space=pltpu.HBM)
    v = pltpu.VMEM
    args = [pltpu.with_memory_space_constraint(a, pltpu.HBM) for a in (attn_out, out_grad, left_old, right_old, basis)]
    return pl.pallas_call(
        kernel,
        out_shape=(
            jax.ShapeDtypeStruct((16, ROWS), F32),
            jax.ShapeDtypeStruct((1, 32, COLS), F32),
            jax.ShapeDtypeStruct((16, COLS), BF16),
        ),
        in_specs=[hbm] * 5,
        out_specs=(vmem, vmem, vmem),
        scratch_shapes=[
            v((TOK, ROWS), BF16),
            v((2 * NC, TOK, W), BF16),
            v((NC, ROWS, W), F32),
            v((NC, ROWS, W), F32),
            v((NC, ROWS, W), F32),
            v((NC, 6, 128, W), F32),
            v((NC, 256, W), F32),
            v((NC, 7, 32, W), F32),
            v((2 * NC, ROWS, W), BF16),
            v((32, COLS), BF16),
            v((4, 512, 128), BF16),
            v((16, ROWS), F32),
            v((32, COLS), F32),
            v((16, ROWS), F32),
            v((4, 16, ROWS), BF16),
            v((256, 128), F32),
            v((256, 128), BF16),
            v((128, ROWS), BF16),
            pltpu.SemaphoreType.DMA((24,)),
            pltpu.SemaphoreType.DMA((44,)),
            pltpu.SemaphoreType.DMA((12,)),
        ],
        compiler_params=pltpu.CompilerParams(
            collective_id=0, has_side_effects=True, vmem_limit_bytes=48 * 1024 * 1024,
        ),
        cost_estimate=pl.CostEstimate(flops=5 * 10**9, bytes_accessed=7 * 2**20, transcendentals=0),
    )(*args)


def solution(mesh):
    return jax.shard_map(
        body,
        mesh=mesh,
        in_specs=(
            P("dp", None),
            P("dp", "mp"),
            P("dp", None),
            P("mp", "dp", None),
            P("mp", "dp", None),
        ),
        out_specs=(P("dp", None), P("mp", "dp", None), P("dp", "mp")),
        check_vma=False,
    )
```

time: 900 us -> 75.1 us (0.08)
  waiting for transfers between devices: 840 us -> 0 us
  Pallas kernels: 0 us -> 72.4 us
  matrix products: 21.7 us -> 0 us
  between operations: 13.8 us -> 0.64 us
  starting transfers between devices: 10.5 us -> 0 us
    reduce_scatter x2 -> x0, waiting for transfers between devices: 591 us -> none  [the longest x1 299 us: body(): lax.psum_scatter(jnp.einsum('tr,tc->rc', attn_out, out_grad, preferred_el...]
    all_gather x2 -> x0, waiting for transfers between devices: 209 us -> none  [the longest x1 110 us: body(): lax.all_gather(columns, 'dp', axis=1, tiled=True)]
    pallas_call x0 -> x1, Pallas kernels: none -> 72.4 us  [body(): pl.pallas_call(kernel, out_shape=(jax.ShapeDtypeStruct((16, ROWS), F32),...]
    psum x1 -> x0, waiting for transfers between devices: 40.4 us -> none  [body(): total = lax.psum(partial_gram, 'mp')]
    dot_general x4 -> x0, matrix products: 21.7 us -> none  [the longest x1 8.94 us: body(): jnp.einsum('tr,tc->rc', attn_out, out_grad, preferred_element_type=jnp.fl...]
    all_to_all x1 -> x0, starting transfers between devices: 10.3 us -> none  [body(): lax.all_to_all(grad_b, 'dp', split_axis=1, concat_axis=0, tiled=True)]
  transfers between devices with their start and end apart: 6 -> 0, of which waited for: 5 -> 0; matrix products, arithmetic and copies ran while one was open for 2% -> 0% of each run, Pallas kernels for 0% -> 0%
where the time goes in v2:
time: 75.1 us; the launch traced here: 75 us
  Pallas kernels  72.4 us (96%)
  local copies, waits for them, and re-layouts  1.96 us (3%)
    pallas_call x1, Pallas kernels, body(): pl.pallas_call(kernel, out_shape=(jax.ShapeDtypeStruct((16, ROWS), F32),...  72.4 us
    unnamed x3, local copies, waits for them, and re-layouts  1.96 us

profile of v2, /device:TPU:1, one launch (start us, length us, event | category | flops | bytes accessed | tf_op | source)
XLA Modules:
  0.0 75.0 jit_solution(1025499569987660315)
XLA Ops:
  0.6 72.4 %shard_map.76 = (f32[16,1024]{1,0:T(8,128)S(1)}, f32[1,32,2048]{2,1,0:T(8,128)S(1)}, bf16[16,2048]{1,0:T(8,128)(2,1)S(1)}) custom-call(bf16[1024,1024]{1,0:T(8,128)(2,1)} %a_hbm.1, bf16[1024,2048]{1,0:T(8,128)(2,1)} %g_hbm.1, f32[16,1024]{1,0:T(8,128)} %left_hbm.1, f32[1,32,2048]{2,1,0:T(8,128)} %right_hbm.1, bf16[1,32,2048]{2,1,0:T(8,128)(2,1)} %basis_hbm.1), custom_call_target="tpu_custom_call" | custom-call | flops 5000000000 | bytes 7340032 | tf_op jit(solution)/shard_map/pallas_call | solution.py:327
  73.0 0.6 copy.11
  73.7 0.7 copy.12
  74.4 0.6 copy.13

commit v3 on v2

--- a/solution.py
+++ b/solution.py
@@ -20,13 +20,12 @@
 EIGHT = [(di, dz) for di in range(4) for dz in range(2) if (di, dz) != (0, 0)]
 
 ORDER = [
-    ("partner", 1), ("own", 0), ("partner", 2), ("own", 1), ("far", 0), ("partner", 3), ("own", 2),
-    ("direct", 0), ("far", 1), ("own", 3), ("aggregate", 0), ("direct", 1), ("far", 2), ("direct", 2),
-    ("far", 3), ("aggregate", 1), ("direct", 3), ("finish", 0), ("aggregate", 2), ("aggregate", 3),
-    ("finish", 1), ("total", 0), ("basis_gather", 0), ("finish", 2), ("finish", 3), ("total", 1), ("gather", 0),
-    ("total", 2), ("total", 3), ("basis_forward", 0), ("forward", 0), ("gather", 1), ("gather", 2), ("end", 0),
-    ("gather", 3), ("basis_end", 0), ("products", 0), ("forward", 1), ("forward", 2), ("forward", 3), ("end", 1),
-    ("end", 2), ("products", 1), ("end", 3), ("products", 2), ("products", 3),
+    ("partner", 1), ("own", 1), ("partner", 2), ("aggregate", 0), ("far", 1), ("own", 2), ("direct", 1), ("far", 2),
+    ("finish", 0), ("basis_gather", 0), ("partner", 3), ("aggregate", 1), ("own", 3), ("direct", 2), ("aggregate", 2),
+    ("far", 3), ("total", 0), ("finish", 1), ("direct", 3), ("aggregate", 3), ("basis_forward", 0), ("finish", 2),
+    ("total", 1), ("gather", 0), ("finish", 3), ("total", 2), ("gather", 1), ("total", 3), ("gather", 2),
+    ("gather", 3), ("basis_end", 0), ("end", 0), ("end", 1), ("end", 2), ("end", 3), ("products", 0), ("products", 1),
+    ("products", 2), ("products", 3),
 ]
 
 
@@ -50,6 +49,7 @@
     s2 = 2 * (1 - c) + 16 * c
     right1 = dp + ((i1 + 1) % 4 - i1) * s1
     left1 = dp + ((i1 + 3) % 4 - i1) * s1
+    opposite1 = dp + ((i1 + 2) % 4 - i1) * s1
     other_core = dp + 1 - 2 * c
     other_z = dp + (1 - 2 * z) * 8
 
@@ -80,15 +80,23 @@
             g_v.at[j if own else NC + j],
         )
 
-    load("a", a_hbm, a_v)
+    def a_load(n):
+        cols = rows(((first_half + n) % 2) * 512, 512, 512)
+        load(("a", n), a_hbm.at[:, cols], a_v.at[:, cols])
+
+    first_half = ((i2 + 2) % 4) // 2
+    a_load(0)
     g_load(False, 0)
+    a_load(1)
     g_load(True, 0)
     load("basis", basis_hbm.at[0], basis_v)
-    for j in range(1, NC):
-        g_load(False, j)
-        g_load(True, j)
-    load("left", left_hbm, left_v)
-    load("right", right_hbm.at[0], right_v)
+
+    def later_loads():
+        for j in range(1, NC):
+            g_load(False, j)
+            g_load(True, j)
+        load("left", left_hbm, left_v)
+        load("right", right_hbm.at[0], right_v)
 
     sent, landed = {}, {}
 
@@ -139,41 +147,72 @@
     def quarter1(i):
         return (i % 4) * 256
 
-    def partner_product(j):
+    def product(dst, g, half):
+        block = rows(half * 512, 512, 512)
+        dst[block, :] = lax.dot_general(
+            a_v[:, block], g[...], (((0,), (0,)), ((), ())), preferred_element_type=F32
+        )
+
+    def both_halves(dst, g):
+        def one(half, carry):
+            product(dst, g, half)
+            return carry
+
+        lax.fori_loop(0, 2, one, 0)
+
+    def partner(j):
         loads[("g", False, j)].wait()
-        p_v[j] = lax.dot_general(a_v[...], g_v[NC + j], (((0,), (0,)), ((), ())), preferred_element_type=F32)
-
-    def partner_send(j):
-        if j == 0:
-            for t in (2, 1, 3, 0):
-                block = rows(quarter1(i2 + t), 256)
-                send(p_v.at[j, block], pr_v.at[j, block], "pair", ("pair", j, t), (other_core, mp))
-        else:
-            send(p_v.at[j], pr_v.at[j], "pair", ("pair", j), (other_core, mp))
-
-    def partner(j):
-        partner_product(j)
-        partner_send(j)
+        both_halves(p_v.at[j], g_v.at[NC + j])
+        send(p_v.at[j], pr_v.at[j], "pair", ("pair", j), (other_core, mp))
 
     def own(j):
         loads[("g", True, j)].wait()
-        o_v[j] = lax.dot_general(a_v[...], g_v[j], (((0,), (0,)), ((), ())), preferred_element_type=F32)
+        both_halves(o_v.at[j], g_v.at[j])
+
+    def first_chunk():
+        p, o = p_v.at[0], o_v.at[0]
+        my_half = ((i1 + 2) % 4) // 2
+        for n in range(2):
+            half = (first_half + n) % 2
+            loads[("a", n)].wait()
+            if n == 0:
+                loads[("g", False, 0)].wait()
+            with jax.named_scope("first"):
+                product(p, g_v.at[NC], half)
+            if n == 0:
+                with jax.named_scope("barrier"):
+                    pl.semaphore_wait(barrier, len(greeted))
+            block = rows(half * 512, 512, 512)
+            send(p.at[block], pr_v.at[0, block], "pair", ("pair", 0, n), (other_core, mp))
+        basis_begin()
+        later_loads()
+        loads[("g", True, 0)].wait()
+        for n in range(2):
+            half = (my_half + n) % 2
+            with jax.named_scope("first"):
+                product(o, g_v.at[0], half)
+            block = rows(half * 512, 512, 512)
+            recv(("pair", 0, n), pr_v.at[0, block])
+            o[block, :] += pr_v[0, block]
+            if n == 0:
+                send_far(0)
+        direct(0)
 
     def part(i, half):
         return rows(quarter1(i) + half * 128, 128)
 
+    def send_far(j):
+        src, land = o_v.at[j], r1_v.at[j]
+        send(src.at[part(i1 + 2, 0)], land.at[0], "ring", ("far", j), (right1, mp))
+        send(src.at[part(i1 + 2, 1)], land.at[1], "ring", ("far", j), (left1, mp))
+
     def far(j):
+        recv(("pair", j), pr_v.at[j])
         for t in (2, 1, 3, 0):
             block = rows(quarter1(i1 + t), 256)
-            if j == 0:
-                recv(("pair", j, t), pr_v.at[j, block])
-            elif t == 2:
-                recv(("pair", j), pr_v.at[j])
             o_v[j, block] += pr_v[j, block]
             if t == 2:
-                src, land = o_v.at[j], r1_v.at[j]
-                send(src.at[part(i1 + 2, 0)], land.at[0], "ring", ("far", j), (right1, mp))
-                send(src.at[part(i1 + 2, 1)], land.at[1], "ring", ("far", j), (left1, mp))
+                send_far(j)
 
     def direct(j):
         src, land = o_v.at[j], r1_v.at[j]
@@ -215,32 +254,27 @@
         buf = cf_v.at[NC * c + j]
         recv(("all8", j), buf.at[rows(quarter1(i1), 224)])
         block = buf.at[rows(quarter1(i1), 256)]
-        send(block, block, ("ring8", j), ("begin", j), (right1, mp))
-        send(block, block, ("ring8", j), ("begin", j), (left1, mp))
+        for device in (right1, left1, opposite1):
+            send(block, block, ("ring4", j), ("ring4", j), (device, mp))
         to_core(j, i1)
 
-    def forward(j):
-        buf = cf_v.at[NC * c + j]
-        recv(("begin", j), buf.at[0:512])
-        half = buf.at[part(i1 + 3, 0)]
-        send(half, half, ("ring8", j), ("forward", j), (right1, mp))
-        half = buf.at[part(i1 + 1, 1)]
-        send(half, half, ("ring8", j), ("forward", j), (left1, mp))
-        to_core(j, i1 + 3)
-        to_core(j, i1 + 1)
-
     def end(j):
-        recv(("forward", j), cf_v.at[NC * c + j, 0:256])
-        to_core(j, i1 + 2)
+        recv(("ring4", j), cf_v.at[NC * c + j, 0:768])
+        for t in (1, 3, 2):
+            to_core(j, i1 + t)
 
     def products(j):
         recv(("core", j), cf_v.at[NC * (1 - c) + j])
 
-        def one(n, carry):
+        def left_one(n, carry):
             k = NC * n + j
             lacc_v[...] += lax.dot_general(
                 cf_v[k, rows(dp * 16, 16)], cf_v[k], (((1,), (1,)), ((), ())), preferred_element_type=F32
             )
+            return carry
+
+        def rotated_one(n, carry):
+            k = NC * n + j
             lhs = jnp.concatenate(
                 [cf_v[k, rows(256 * xx + 128 * z + 32 * yy + 16 * c, 16)] for xx in range(4) for yy in range(4)], 0
             )
@@ -250,32 +284,26 @@
             racc_v[...] += jnp.dot(lhs, rhs, preferred_element_type=F32)
             return carry
 
-        lax.fori_loop(0, 2, one, 0)
+        lax.fori_loop(0, 2, left_one, 0)
+        if j == NC - 1:
+            lr_v[mp] = lacc_v[...].astype(BF16)
+            for d in range(1, 4):
+                send(lr_v.at[mp], lr_v.at[mp], "left", "left", (dp, (mp + d) % 4))
+        lax.fori_loop(0, 2, rotated_one, 0)
 
     steps = {
         "partner": partner, "own": own, "far": far, "direct": direct, "aggregate": aggregate, "finish": finish,
-        "total": total, "gather": gather, "forward": forward, "end": end, "products": products,
+        "total": total, "gather": gather, "end": end, "products": products,
         "basis_gather": lambda j: basis_gather(), "basis_forward": lambda j: basis_forward(),
         "basis_end": lambda j: basis_end(),
     }
 
-    loads["a"].wait()
-    with jax.named_scope("first"):
-        partner_product(0)
-        lacc_v[...] = jnp.zeros_like(lacc_v)
-        racc_v[...] = jnp.zeros_like(racc_v)
-    with jax.named_scope("barrier"):
-        pl.semaphore_wait(barrier, len(greeted))
-    partner_send(0)
-    basis_begin()
+    first_chunk()
+    lacc_v[...] = jnp.zeros_like(lacc_v)
+    racc_v[...] = jnp.zeros_like(racc_v)
     for step, j in ORDER:
         with jax.named_scope(f"{step}_{j}"):
             steps[step](j)
-
-    with jax.named_scope("left_send"):
-        lr_v[mp] = lacc_v[...].astype(BF16)
-        for d in range(1, 4):
-            send(lr_v.at[mp], lr_v.at[mp], "left", "left", (dp, (mp + d) % 4))
 
     with jax.named_scope("rotated_send"):
         rsend_v[...] = racc_v[...].astype(BF16)
@@ -297,19 +325,6 @@
 
         lax.fori_loop(0, 2 * NC, right_step, 0)
 
-    with jax.named_scope("sent"):
-        wait_sent("pair", p_v)
-        wait_sent("ring", r1_v)
-        wait_sent("eight", r2_v)
-        for j in range(NC):
-            wait_sent(("all8", j), cf_v.at[0, 0:224])
-            wait_sent(("ring8", j), cf_v.at[0, 0:768])
-            wait_sent(("core", j), cf_v.at[0])
-        wait_sent("basis", bp_v.at[0, 0:480])
-        for name in ("basis_core", "basis_z", "basis_forward"):
-            wait_sent(name, bp_v.at[0])
-        wait_sent("rotated", rsend_v.at[0:240])
-        wait_sent("left", lr_v.at[0:3])
     with jax.named_scope("rotated_recv"):
         recv("rotated", rsend_v.at[0:240])
     with jax.named_scope("left_recv"):
@@ -317,6 +332,19 @@
         recv("left", lr_v.at[0:3])
         gram = lr_v[0].astype(F32) + lr_v[1].astype(F32) + lr_v[2].astype(F32) + lr_v[3].astype(F32)
         left_out[...] = 0.9 * left_v[...] + 0.1 * (gram / (4 * COLS))
+    with jax.named_scope("sent"):
+        wait_sent("pair", p_v)
+        wait_sent("ring", r1_v)
+        wait_sent("eight", r2_v)
+        for j in range(NC):
+            wait_sent(("all8", j), cf_v.at[0, 0:224])
+            wait_sent(("ring4", j), cf_v.at[0, 0:768])
+            wait_sent(("core", j), cf_v.at[0])
+        wait_sent("basis", bp_v.at[0, 0:480])
+        for name in ("basis_core", "basis_z", "basis_forward"):
+            wait_sent(name, bp_v.at[0])
+        wait_sent("rotated", rsend_v.at[0:240])
+        wait_sent("left", lr_v.at[0:3])
 
 
 def body(attn_out, out_grad, left_old, right_old, basis):
@@ -324,13 +352,14 @@
     hbm = pl.BlockSpec(memory_space=pltpu.HBM)
     v = pltpu.VMEM
     args = [pltpu.with_memory_space_constraint(a, pltpu.HBM) for a in (attn_out, out_grad, left_old, right_old, basis)]
+    shapes = (
+        jax.ShapeDtypeStruct((16, ROWS), F32),
+        jax.ShapeDtypeStruct((1, 32, COLS), F32),
+        jax.ShapeDtypeStruct((16, COLS), BF16),
+    )
     return pl.pallas_call(
         kernel,
-        out_shape=(
-            jax.ShapeDtypeStruct((16, ROWS), F32),
-            jax.ShapeDtypeStruct((1, 32, COLS), F32),
-            jax.ShapeDtypeStruct((16, COLS), BF16),
-        ),
+        out_shape=shapes,
         in_specs=[hbm] * 5,
         out_specs=(vmem, vmem, vmem),
         scratch_shapes=[
@@ -352,9 +381,9 @@
             v((256, 128), F32),
             v((256, 128), BF16),
             v((128, ROWS), BF16),
-            pltpu.SemaphoreType.DMA((24,)),
-            pltpu.SemaphoreType.DMA((44,)),
-            pltpu.SemaphoreType.DMA((12,)),
+            pltpu.SemaphoreType.DMA((21,)),
+            pltpu.SemaphoreType.DMA((36,)),
+            pltpu.SemaphoreType.DMA((13,)),
         ],
         compiler_params=pltpu.CompilerParams(
             collective_id=0, has_side_effects=True, vmem_limit_bytes=48 * 1024 * 1024,

time: 75.1 us -> 68.5 us (0.912)
  Pallas kernels: 72.4 us -> 65.8 us
    pallas_call x1, Pallas kernels: 72.4 us -> 65.8 us  [body(): pl.pallas_call(kernel, out_shape=shapes, in_specs=[hbm] * 5, out_specs=(v...]
where the time goes in v3:
time: 68.5 us; the launch traced here: 68.4 us
  Pallas kernels  65.8 us (96%)
  local copies, waits for them, and re-layouts  1.96 us (3%)
    pallas_call x1, Pallas kernels, body(): pl.pallas_call(kernel, out_shape=shapes, in_specs=[hbm] * 5, out_specs=(v...  65.8 us
    unnamed x3, local copies, waits for them, and re-layouts  1.96 us

profile of v3, /device:TPU:1, one launch (start us, length us, event | category | flops | bytes accessed | tf_op | source)
XLA Modules:
  0.0 68.4 jit_solution(8130916976073816125)
XLA Ops:
  0.6 65.8 %shard_map.76 = (f32[16,1024]{1,0:T(8,128)S(1)}, f32[1,32,2048]{2,1,0:T(8,128)S(1)}, bf16[16,2048]{1,0:T(8,128)(2,1)S(1)}) custom-call(bf16[1024,1024]{1,0:T(8,128)(2,1)} %a_hbm.1, bf16[1024,2048]{1,0:T(8,128)(2,1)} %g_hbm.1, f32[16,1024]{1,0:T(8,128)} %left_hbm.1, f32[1,32,2048]{2,1,0:T(8,128)} %right_hbm.1, bf16[1,32,2048]{2,1,0:T(8,128)(2,1)} %basis_hbm.1), custom_call_target="tpu_custom_call" | custom-call | flops 5000000000 | bytes 7340032 | tf_op jit(solution)/shard_map/pallas_call | solution.py:360
  66.5 0.6 copy.11
  67.1 0.7 %copy.12 = f32[1,32,2048]{2,1,0:T(8,128)} copy(f32[1,32,2048]{2,1,0:T(8,128)S(1)} %get-tuple-element.7) | data formatting | bytes 524288
  67.8 0.6 copy.13

commit v4 on v3

v4 whole, which is shorter than its diff:
```python
import jax
import jax.numpy as jnp
from jax import lax
from jax.experimental import pallas as pl
from jax.experimental.pallas import tpu as pltpu
from jax.sharding import PartitionSpec as P

MESH = pl.DeviceIdType.MESH
F32 = jnp.float32
BF16 = jnp.bfloat16

ROWS = 1024
TOK = 1024
COLS = 2048
HALF = 1024

CHUNKS = [(0, 256, False), (256, 256, False), (512, 128, False), (640, 128, False), (768, 128, True), (896, 128, True)]
TOGETHER = {0: (0,), 1: (1,), 2: (2, 3), 4: (4, 5)}
SEND_SEMS, RECV_SEMS, LOAD_SEMS = 42, 53, 13

PLANE = [(dx, dy) for dx in range(4) for dy in range(4) if (dx, dy) != (0, 0)]
EIGHT = [(di, dz) for di in range(4) for dz in range(2) if (di, dz) != (0, 0)]

ORDER = [
    ("partner", 2), ("own", 2), ("partner", 1), ("aggregate", 0), ("partner", 4), ("far", 2), ("direct", 2),
    ("own", 4), ("far", 3), ("direct", 3), ("finish", 0), ("basis_gather", 0), ("own", 1), ("far", 1),
    ("aggregate", 3), ("direct", 1), ("far", 5), ("aggregate", 2), ("aggregate", 1), ("far", 4), ("direct", 5),
    ("finish", 3), ("total", 0), ("aggregate", 5), ("finish", 2), ("finish", 1), ("direct", 4), ("aggregate", 4),
    ("basis_forward", 0), ("total", 3), ("finish", 5), ("total", 2), ("total", 1), ("gather", 0), ("finish", 4),
    ("total", 5), ("gather", 3), ("gather", 2), ("gather", 1), ("total", 4), ("forward", 0), ("forward", 3),
    ("gather", 5), ("forward", 2), ("forward", 1), ("gather", 4), ("end", 0), ("end", 3), ("end", 2), ("end", 5),
    ("basis_end", 0), ("products", 3), ("end", 1), ("products", 0), ("end", 4), ("products", 2), ("products", 5),
    ("products", 1), ("products", 4),
]


def rows(start, size, unit=16):
    return pl.ds(pl.multiple_of(start, unit), size)


def kernel(
    a_hbm, g_hbm, left_hbm, right_hbm, basis_hbm, left_out, right_out, rot_out,
    a_v, g_v, p_v, pr_v, o_v, r1_v, t1_v, r2_v, cf_v,
    basis_v, bp_v, left_v, right_v, lacc_v, lr_v, racc_v, rsend_v, ct_v,
    ssem, rsem, lsem,
):
    dp = lax.axis_index("dp")
    mp = lax.axis_index("mp")
    x, z, y, c = dp // 16, (dp // 8) % 2, (dp // 2) % 4, dp % 2
    i1 = x * (1 - c) + y * c
    i2 = y * (1 - c) + x * c
    s1 = 16 * (1 - c) + 2 * c
    s2 = 2 * (1 - c) + 16 * c
    right1 = dp + ((i1 + 1) % 4 - i1) * s1
    left1 = dp + ((i1 + 3) % 4 - i1) * s1
    opposite1 = dp + ((i1 + 2) % 4 - i1) * s1
    other_core = dp + 1 - 2 * c
    other_z = dp + (1 - 2 * z) * 8

    def plane(dx, dy):
        return ((x + dx) % 4) * 16 + z * 8 + ((y + dy) % 4) * 2 + c

    def eight(di, dz):
        return dp + ((i2 + di) % 4 - i2) * s2 + ((z + dz) % 2 - z) * 8

    loads = {}

    def load(name, src, dst):
        copy = pltpu.make_async_copy(src, dst, lsem.at[len(loads)])
        copy.start()
        loads[name] = copy

    def g_load(own, head):
        half = c if own else 1 - c
        load(
            ("g", own, head),
            g_hbm.at[:, rows(half * HALF + CHUNKS[head][0], 256, 128)],
            g_v[2 * list(TOGETHER).index(head) + own],
        )

    def a_load(n):
        cols = rows(((first_half + n) % 2) * 512, 512, 512)
        load(("a", n), a_hbm.at[:, cols], a_v.at[:, cols])

    first_half = ((i2 + 2) % 4) // 2
    a_load(0)
    g_load(False, 0)
    a_load(1)
    g_load(True, 0)
    load("basis", basis_hbm.at[0], basis_v)

    barrier = pltpu.get_barrier_semaphore()
    greeted = [(plane(dx, dy), mp) for dx, dy in PLANE] + [(eight(di, 1), mp) for di in range(4)]
    greeted += [(other_core, mp)] + [(dp, (mp + d) % 4) for d in range(1, 4)]
    for device in greeted:
        pl.semaphore_signal(barrier, inc=1, device_id=device, device_id_type=MESH)

    def later_loads():
        for head in list(TOGETHER)[1:]:
            g_load(False, head)
            g_load(True, head)
        load("left", left_hbm, left_v)
        load("right", right_hbm.at[0], right_v)

    sent, landed = {}, {}

    def descriptor(src, dst, out, into, device):
        return pltpu.make_async_remote_copy(
            src_ref=src, dst_ref=dst,
            send_sem=ssem.at[sent.setdefault(out, len(sent))],
            recv_sem=rsem.at[landed.setdefault(into, len(landed))],
            device_id=device, device_id_type=MESH,
        )

    def send(src, dst, out, into, device):
        descriptor(src, dst, out, into, device).start()

    def recv(into, span):
        pltpu.make_async_copy(span, span, rsem.at[landed[into]]).wait()

    def wait_sent(out, span):
        pltpu.make_async_copy(span, span, ssem.at[sent[out]]).wait()

    p_me = 4 * x + y
    zc = 2 * z + c

    def basis_begin():
        loads["basis"].wait()
        for dx, dy in PLANE:
            p_to = 4 * ((x + dx) % 4) + (y + dy) % 4
            send(
                basis_v.at[:, rows(p_to * 128, 128, 128)], bp_v.at[zc, rows(p_me * 32, 32)],
                "basis", "basis", (plane(dx, dy), mp),
            )
        bp_v[zc, rows(p_me * 32, 32)] = basis_v[:, rows(p_me * 128, 128, 128)]

    def basis_gather():
        recv("basis", bp_v.at[zc, 0:480])
        send(bp_v.at[zc], bp_v.at[zc], "basis_core", "basis_core", (other_core, mp))
        send(bp_v.at[zc], bp_v.at[zc], "basis_z", "basis_z", (other_z, mp))

    def basis_forward():
        from_z = 2 * (1 - z) + c
        recv("basis_z", bp_v.at[from_z])
        send(bp_v.at[from_z], bp_v.at[from_z], "basis_forward", "basis_forward", (other_core, mp))

    def basis_end():
        recv("basis_core", bp_v.at[2 * z + 1 - c])
        recv("basis_forward", bp_v.at[2 * (1 - z) + 1 - c])

    def quarter1(i):
        return (i % 4) * 256

    def product(refs, own, head, half):
        block = rows(half * 512, 512, 512)
        value = lax.dot_general(
            a_v[:, block], g_v[2 * list(TOGETHER).index(head) + own][...], (((0,), (0,)), ((), ())),
            preferred_element_type=F32,
        )
        for j in TOGETHER[head]:
            start = CHUNKS[j][0] - CHUNKS[head][0]
            refs[j][block, :] = value[:, start:start + CHUNKS[j][1]]

    def both_halves(refs, own, head):
        loads[("g", own, head)].wait()

        def one(half, carry):
            product(refs, own, head, half)
            return carry

        lax.fori_loop(0, 2, one, 0)

    def partner(head):
        both_halves(p_v, False, head)
        for j in TOGETHER[head]:
            send(p_v[j], pr_v[j], ("pair", j), ("pair", j), (other_core, mp))

    def own(head):
        both_halves(o_v, True, head)

    def first_chunk():
        p, o = p_v[0], o_v[0]
        my_half = ((i1 + 2) % 4) // 2
        for n in range(2):
            half = (first_half + n) % 2
            loads[("a", n)].wait()
            if n == 0:
                loads[("g", False, 0)].wait()
            with jax.named_scope("first"):
                product(p_v, False, 0, half)
            if n == 0:
                with jax.named_scope("barrier"):
                    pl.semaphore_wait(barrier, len(greeted))
            block = rows(half * 512, 512, 512)
            send(p.at[block], pr_v[0].at[block], ("pair", 0), ("pair", 0, n), (other_core, mp))
        basis_begin()
        later_loads()
        loads[("g", True, 0)].wait()
        for n in range(2):
            half = (my_half + n) % 2
            with jax.named_scope("first"):
                product(o_v, True, 0, half)
            block = rows(half * 512, 512, 512)
            recv(("pair", 0, n), pr_v[0].at[block])
            o[block, :] += pr_v[0][block, :]
            if n == 0:
                send_far(0)
        direct(0)

    def part(i, half):
        return rows(quarter1(i) + half * 128, 128)

    def send_far(j):
        src, land = o_v[j], r1_v[j]
        send(src.at[part(i1 + 2, 0)], land.at[0], ("ring", j), ("far", j), (right1, mp))
        send(src.at[part(i1 + 2, 1)], land.at[1], ("ring", j), ("far", j), (left1, mp))

    def far(j):
        recv(("pair", j), pr_v[j])
        for t in (2, 1, 3, 0):
            block = rows(quarter1(i1 + t), 256)
            o_v[j][block, :] += pr_v[j][block, :]
            if t == 2:
                send_far(j)

    def direct(j):
        src, land = o_v[j], r1_v[j]
        send(src.at[part(i1 + 1, 1)], land.at[2], ("ring", j), ("near", j), (right1, mp))
        send(src.at[part(i1 + 3, 0)], land.at[3], ("ring", j), ("near", j), (left1, mp))

    def aggregate(j):
        src, land = o_v[j], r1_v[j]
        recv(("far", j), land.at[0:2])
        src[part(i1 + 1, 0), :] += land[0]
        send(src.at[part(i1 + 1, 0)], land.at[4], ("ring", j), ("near", j), (right1, mp))
        src[part(i1 + 3, 1), :] += land[1]
        send(src.at[part(i1 + 3, 1)], land.at[5], ("ring", j), ("near", j), (left1, mp))

    def finish(j):
        src, land, dst = o_v[j], r1_v[j], t1_v[j]
        recv(("near", j), land.at[2:6])
        dst[0:128, :] = src[part(i1, 0), :] + land[3] + land[4]
        dst[128:256, :] = src[part(i1, 1), :] + land[2] + land[5]
        for n, (di, dz) in enumerate(EIGHT):
            block = rows(((i2 + di) % 4) * 64 + ((z + dz) % 2) * 32, 32)
            send(dst.at[block], r2_v[j].at[n], ("eight", j), ("eight", j), (eight(di, dz), mp))

    def total(j):
        recv(("eight", j), r2_v[j])
        value = t1_v[j][rows(i2 * 64 + z * 32, 32), :]
        for n in range(len(EIGHT)):
            value += r2_v[j][n]
        mine = cf_v[j].at[c, rows(i1 * 256 + i2 * 64 + z * 32, 32)]
        mine[...] = value.astype(BF16)
        for di, dz in EIGHT:
            send(mine, mine, ("all8", j), ("all8", j), (eight(di, dz), mp))

    def to_core(j, i):
        block = cf_v[j].at[c, rows(quarter1(i), 256)]
        send(block, block, ("core", j), ("core", j), (other_core, mp))

    def gather(j):
        buf = cf_v[j].at[c]
        recv(("all8", j), buf.at[rows(quarter1(i1), 224)])
        block = buf.at[rows(quarter1(i1), 256)]
        for device in (right1, left1) + ((opposite1,) if CHUNKS[j][2] else ()):
            send(block, block, ("four", j), ("begin", j), (device, mp))
        to_core(j, i1)

    def forward(j):
        buf = cf_v[j].at[c]
        recv(("begin", j), buf.at[0:512])
        half = buf.at[part(i1 + 3, 0)]
        send(half, half, ("four", j), ("forward", j), (right1, mp))
        half = buf.at[part(i1 + 1, 1)]
        send(half, half, ("four", j), ("forward", j), (left1, mp))
        to_core(j, i1 + 3)
        to_core(j, i1 + 1)

    def end(j):
        buf = cf_v[j].at[c]
        if CHUNKS[j][2]:
            recv(("begin", j), buf.at[0:768])
            to_core(j, i1 + 3)
            to_core(j, i1 + 1)
        else:
            recv(("forward", j), buf.at[0:256])
        to_core(j, i1 + 2)

    done = []

    def products(j):
        start, width, _ = CHUNKS[j]
        cf = cf_v[j]
        recv(("core", j), cf.at[1 - c])
        done.append(j)

        def left_one(n):
            return lax.dot_general(
                cf[n, rows(dp * 16, 16)], cf[n], (((1,), (1,)), ((), ())), preferred_element_type=F32
            )

        def rotated_one(n):
            lhs = jnp.concatenate(
                [cf[n, rows(256 * xx + 128 * z + 32 * yy + 16 * c, 16)] for xx in range(4) for yy in range(4)], 0
            )
            holders = [32 * n + start // 32 + b for b in range(width // 32)]
            rhs = jnp.concatenate(
                [bp_v[2 * ((h // 8) % 2) + h % 2, rows((4 * (h // 16) + (h // 2) % 4) * 32, 32)] for h in holders], 0
            )
            return jnp.dot(lhs, rhs, preferred_element_type=F32)

        lacc_v[...] += left_one(0) + left_one(1)
        if len(done) == len(CHUNKS):
            lr_v[mp] = lacc_v[...].astype(BF16)
            for d in range(1, 4):
                send(lr_v.at[mp], lr_v.at[mp], "left", "left", (dp, (mp + d) % 4))
        racc_v[...] += rotated_one(0) + rotated_one(1)

    steps = {
        "partner": partner, "own": own, "far": far, "direct": direct, "aggregate": aggregate, "finish": finish,
        "total": total, "gather": gather, "forward": forward, "end": end, "products": products,
        "basis_gather": lambda j: basis_gather(), "basis_forward": lambda j: basis_forward(),
        "basis_end": lambda j: basis_end(),
    }

    first_chunk()
    lacc_v[...] = jnp.zeros_like(lacc_v)
    racc_v[...] = jnp.zeros_like(racc_v)
    for step, j in ORDER:
        with jax.named_scope(f"{step}_{j}"):
            steps[step](j)

    with jax.named_scope("rotated_send"):
        rsend_v[...] = racc_v[...].astype(BF16)
        mine = rows(p_me * 128, 128, 128)
        for dx, dy in PLANE:
            p_to = 4 * ((x + dx) % 4) + (y + dy) % 4
            send(rsend_v.at[rows(p_to * 16, 16)], rot_out.at[:, mine], "rotated", "rotated", (plane(dx, dy), mp))
        rot_out[:, mine] = rsend_v[rows(p_me * 16, 16), :]

    with jax.named_scope("right"):
        column = 32 * (dp % 32)
        for j, (start, width, _) in enumerate(CHUNKS):
            @pl.when((column >= start) & (column < start + width))
            def _():
                ct_v[...] = cf_v[j][dp // 32, :, rows(((column - start) // 128) * 128, 128, 128)].T
        loads["right"].wait()
        for j, (start, width, _) in enumerate(CHUNKS):
            for n in range(2):
                cols = rows(n * HALF + start, width, 128)
                gram = jnp.dot(ct_v[rows(32 * (dp % 4), 32), :], cf_v[j][n], preferred_element_type=F32)
                right_out[0, :, cols] = 0.9 * right_v[:, cols] + 0.1 * (gram / ROWS)

    with jax.named_scope("rotated_recv"):
        recv("rotated", rsend_v.at[0:240])
    with jax.named_scope("left_recv"):
        loads["left"].wait()
        recv("left", lr_v.at[0:3])
        gram = lr_v[0].astype(F32) + lr_v[1].astype(F32) + lr_v[2].astype(F32) + lr_v[3].astype(F32)
        left_out[...] = 0.9 * left_v[...] + 0.1 * (gram / (4 * COLS))
    with jax.named_scope("sent"):
        for j in range(len(CHUNKS)):
            wait_sent(("pair", j), p_v[j])
            wait_sent(("ring", j), r1_v[j])
            wait_sent(("eight", j), r2_v[j])
            wait_sent(("all8", j), cf_v[j].at[0, 0:224])
            wait_sent(("four", j), cf_v[j].at[0, 0:768])
            wait_sent(("core", j), cf_v[j].at[0])
        wait_sent("basis", bp_v.at[0, 0:480])
        for name in ("basis_core", "basis_z", "basis_forward"):
            wait_sent(name, bp_v.at[0])
        wait_sent("rotated", rsend_v.at[0:240])
        wait_sent("left", lr_v.at[0:3])


def write_out(*refs):
    sources, results, sems = refs[:3], refs[3:6], refs[6]
    copies = [pltpu.make_async_copy(a, b, sems.at[n]) for n, (a, b) in enumerate(zip(sources, results))]
    for copy in copies:
        copy.start()
    for copy in copies:
        copy.wait()


def body(attn_out, out_grad, left_old, right_old, basis):
    vmem = pl.BlockSpec(memory_space=pltpu.VMEM)
    hbm = pl.BlockSpec(memory_space=pltpu.HBM)
    v = pltpu.VMEM
    args = [pltpu.with_memory_space_constraint(a, pltpu.HBM) for a in (attn_out, out_grad, left_old, right_old, basis)]
    shapes = (
        jax.ShapeDtypeStruct((16, ROWS), F32),
        jax.ShapeDtypeStruct((1, 32, COLS), F32),
        jax.ShapeDtypeStruct((16, COLS), BF16),
    )
    shapes = (
        jax.ShapeDtypeStruct((16, ROWS), F32),
        jax.ShapeDtypeStruct((1, 32, COLS), F32),
        jax.ShapeDtypeStruct((16, COLS), BF16),
    )
    results = pl.pallas_call(
        kernel,
        out_shape=tuple(pltpu.VMEM(q.shape, q.dtype) for q in shapes),
        in_specs=[hbm] * 5,
        out_specs=(vmem, vmem, vmem),
        scratch_shapes=[
            v((TOK, ROWS), BF16),
            [v((TOK, 256), BF16) for _ in range(2 * len(TOGETHER))],
            [v((ROWS, w), F32) for _, w, _ in CHUNKS],
            [v((ROWS, w), F32) for _, w, _ in CHUNKS],
            [v((ROWS, w), F32) for _, w, _ in CHUNKS],
            [v((6, 128, w), F32) for _, w, _ in CHUNKS],
            [v((256, w), F32) for _, w, _ in CHUNKS],
            [v((7, 32, w), F32) for _, w, _ in CHUNKS],
            [v((2, ROWS, w), BF16) for _, w, _ in CHUNKS],
            v((32, COLS), BF16),
            v((4, 512, 128), BF16),
            v((16, ROWS), F32),
            v((32, COLS), F32),
            v((16, ROWS), F32),
            v((4, 16, ROWS), BF16),
            v((256, 128), F32),
            v((256, 128), BF16),
            v((128, ROWS), BF16),
            pltpu.SemaphoreType.DMA((SEND_SEMS,)),
            pltpu.SemaphoreType.DMA((RECV_SEMS,)),
            pltpu.SemaphoreType.DMA((LOAD_SEMS,)),
        ],
        compiler_params=pltpu.CompilerParams(
            collective_id=0, has_side_effects=True, vmem_limit_bytes=48 * 1024 * 1024,
        ),
        cost_estimate=pl.CostEstimate(flops=5 * 10**9, bytes_accessed=7 * 2**20, transcendentals=0),
    )(*args)
    return pl.pallas_call(
        write_out,
        out_shape=shapes,
        in_specs=[vmem] * 3,
        out_specs=(hbm,) * 3,
        scratch_shapes=[pltpu.SemaphoreType.DMA((3,))],
    )(*(pltpu.with_memory_space_constraint(r, pltpu.VMEM) for r in results))


def solution(mesh):
    return jax.shard_map(
        body,
        mesh=mesh,
        in_specs=(
            P("dp", None),
            P("dp", "mp"),
            P("dp", None),
            P("mp", "dp", None),
            P("mp", "dp", None),
        ),
        out_specs=(P("dp", None), P("mp", "dp", None), P("dp", "mp")),
        check_vma=False,
    )
```

time: 68.5 us -> 65.8 us (0.961)
  local copies, waits for them, and re-layouts: 1.96 us -> 0 us
  Pallas kernels: 65.8 us -> 65 us
    unnamed x3 -> x0, local copies, waits for them, and re-layouts: 1.96 us -> none
    pallas_call x1 -> x2, Pallas kernels: 65.8 us -> 65 us  [the longest x1 64.3 us: body(): pl.pallas_call(kernel, out_shape=tuple((pltpu.VMEM(q.shape, q.dtype) for...]
where the time goes in v4:
time: 65.8 us; the launch traced here: 65.7 us
  Pallas kernels  65 us (99%)
    pallas_call x1, Pallas kernels, body(): pl.pallas_call(kernel, out_shape=tuple((pltpu.VMEM(q.shape, q.dtype) for...  64.3 us

profile of v4, /device:TPU:1, one launch (start us, length us, event | category | flops | bytes accessed | tf_op | source)
XLA Modules:
  0.0 65.7 jit_solution(8973429425750249096)
XLA Ops:
  0.6 64.3 %shard_map.76 = (f32[16,1024]{1,0:T(8,128)S(1)}, f32[1,32,2048]{2,1,0:T(8,128)S(1)}, bf16[16,2048]{1,0:T(8,128)(2,1)S(1)}) custom-call(bf16[1024,1024]{1,0:T(8,128)(2,1)} %a_hbm.1, bf16[1024,2048]{1,0:T(8,128)(2,1)} %g_hbm.1, f32[16,1024]{1,0:T(8,128)} %left_hbm.1, f32[1,32,2048]{2,1,0:T(8,128)} %right_hbm.1, bf16[1,32,2048]{2,1,0:T(8,128)(2,1)} %basis_hbm.1), custom_call_target="tpu_custom_call" | custom-call | flops 5000000000 | bytes 7340032 | tf_op jit(solution)/shard_map/pallas_call | solution.py:401
  64.9 0.8 %shard_map.77 = (f32[16,1024]{1,0:T(8,128)}, f32[1,32,2048]{2,1,0:T(8,128)}, bf16[16,2048]{1,0:T(8,128)(2,1)}) custom-call(f32[16,1024]{1,0:T(8,128)S(1)} %get-tuple-element.6.refs_0_, f32[1,32,2048]{2,1,0:T(8,128)S(1)} %get-tuple-element.7.refs_1_, bf16[16,2048]{1,0:T(8,128)(2,1)S(1)} %get-tuple-element.8.refs_2_), custom_call_target="tpu_custom_call" | custom-call | tf_op jit(solution)/shard_map/pallas_call | solution.py:434

commit v5 on v4

--- a/solution.py
+++ b/solution.py
@@ -14,23 +14,23 @@
 COLS = 2048
 HALF = 1024
 
-CHUNKS = [(0, 256, False), (256, 256, False), (512, 128, False), (640, 128, False), (768, 128, True), (896, 128, True)]
+CHUNKS = [(0, 256, False), (256, 256, False), (512, 128, True), (640, 128, True), (768, 128, False), (896, 128, False)]
 TOGETHER = {0: (0,), 1: (1,), 2: (2, 3), 4: (4, 5)}
-SEND_SEMS, RECV_SEMS, LOAD_SEMS = 42, 53, 13
+SEND_SEMS, RECV_SEMS, LOAD_SEMS = 14, 53, 13
 
 PLANE = [(dx, dy) for dx in range(4) for dy in range(4) if (dx, dy) != (0, 0)]
 EIGHT = [(di, dz) for di in range(4) for dz in range(2) if (di, dz) != (0, 0)]
 
 ORDER = [
-    ("partner", 2), ("own", 2), ("partner", 1), ("aggregate", 0), ("partner", 4), ("far", 2), ("direct", 2),
-    ("own", 4), ("far", 3), ("direct", 3), ("finish", 0), ("basis_gather", 0), ("own", 1), ("far", 1),
-    ("aggregate", 3), ("direct", 1), ("far", 5), ("aggregate", 2), ("aggregate", 1), ("far", 4), ("direct", 5),
-    ("finish", 3), ("total", 0), ("aggregate", 5), ("finish", 2), ("finish", 1), ("direct", 4), ("aggregate", 4),
-    ("basis_forward", 0), ("total", 3), ("finish", 5), ("total", 2), ("total", 1), ("gather", 0), ("finish", 4),
-    ("total", 5), ("gather", 3), ("gather", 2), ("gather", 1), ("total", 4), ("forward", 0), ("forward", 3),
-    ("gather", 5), ("forward", 2), ("forward", 1), ("gather", 4), ("end", 0), ("end", 3), ("end", 2), ("end", 5),
-    ("basis_end", 0), ("products", 3), ("end", 1), ("products", 0), ("end", 4), ("products", 2), ("products", 5),
-    ("products", 1), ("products", 4),
+    ("partner", 4), ("own", 4), ("partner", 1), ("aggregate", 0), ("partner", 2), ("far", 4), ("far", 5),
+    ("direct", 5), ("direct", 4), ("own", 1), ("far", 1), ("finish", 0), ("basis_gather", 0), ("aggregate", 5),
+    ("direct", 1), ("own", 2), ("aggregate", 1), ("total", 0), ("far", 2), ("finish", 5), ("far", 3),
+    ("aggregate", 4), ("finish", 1), ("direct", 2), ("aggregate", 2), ("direct", 3), ("aggregate", 3),
+    ("basis_forward", 0), ("finish", 4), ("total", 1), ("total", 5), ("gather", 0), ("finish", 3), ("total", 4),
+    ("finish", 2), ("gather", 1), ("gather", 5), ("total", 3), ("forward", 0), ("gather", 4), ("total", 2),
+    ("forward", 1), ("forward", 5), ("gather", 3), ("forward", 4), ("gather", 2), ("end", 0), ("end", 1), ("end", 5),
+    ("end", 3), ("end", 4), ("basis_end", 0), ("products", 1), ("end", 2), ("products", 0), ("products", 5),
+    ("products", 4), ("products", 3), ("products", 2),
 ]
 
 
@@ -173,7 +173,7 @@
     def partner(head):
         both_halves(p_v, False, head)
         for j in TOGETHER[head]:
-            send(p_v[j], pr_v[j], ("pair", j), ("pair", j), (other_core, mp))
+            send(p_v[j], pr_v[j], ("pair", CHUNKS[j][0] // 512), ("pair", j), (other_core, mp))
 
     def own(head):
         both_halves(o_v, True, head)
@@ -212,8 +212,8 @@
 
     def send_far(j):
         src, land = o_v[j], r1_v[j]
-        send(src.at[part(i1 + 2, 0)], land.at[0], ("ring", j), ("far", j), (right1, mp))
-        send(src.at[part(i1 + 2, 1)], land.at[1], ("ring", j), ("far", j), (left1, mp))
+        send(src.at[part(i1 + 2, 0)], land.at[0], ("ring", CHUNKS[j][0] // 512), ("far", j), (right1, mp))
+        send(src.at[part(i1 + 2, 1)], land.at[1], ("ring", CHUNKS[j][0] // 512), ("far", j), (left1, mp))
 
     def far(j):
         recv(("pair", j), pr_v[j])
@@ -225,16 +225,16 @@
 
     def direct(j):
         src, land = o_v[j], r1_v[j]
-        send(src.at[part(i1 + 1, 1)], land.at[2], ("ring", j), ("near", j), (right1, mp))
-        send(src.at[part(i1 + 3, 0)], land.at[3], ("ring", j), ("near", j), (left1, mp))
+        send(src.at[part(i1 + 1, 1)], land.at[2], ("ring", CHUNKS[j][0] // 512), ("near", j), (right1, mp))
+        send(src.at[part(i1 + 3, 0)], land.at[3], ("ring", CHUNKS[j][0] // 512), ("near", j), (left1, mp))
 
     def aggregate(j):
         src, land = o_v[j], r1_v[j]
         recv(("far", j), land.at[0:2])
         src[part(i1 + 1, 0), :] += land[0]
-        send(src.at[part(i1 + 1, 0)], land.at[4], ("ring", j), ("near", j), (right1, mp))
+        send(src.at[part(i1 + 1, 0)], land.at[4], ("ring", CHUNKS[j][0] // 512), ("near", j), (right1, mp))
         src[part(i1 + 3, 1), :] += land[1]
-        send(src.at[part(i1 + 3, 1)], land.at[5], ("ring", j), ("near", j), (left1, mp))
+        send(src.at[part(i1 + 3, 1)], land.at[5], ("ring", CHUNKS[j][0] // 512), ("near", j), (left1, mp))
 
     def finish(j):
         src, land, dst = o_v[j], r1_v[j], t1_v[j]
@@ -243,7 +243,7 @@
         dst[128:256, :] = src[part(i1, 1), :] + land[2] + land[5]
         for n, (di, dz) in enumerate(EIGHT):
             block = rows(((i2 + di) % 4) * 64 + ((z + dz) % 2) * 32, 32)
-            send(dst.at[block], r2_v[j].at[n], ("eight", j), ("eight", j), (eight(di, dz), mp))
+            send(dst.at[block], r2_v[j].at[n], "eight", ("eight", j), (eight(di, dz), mp))
 
     def total(j):
         recv(("eight", j), r2_v[j])
@@ -253,27 +253,27 @@
         mine = cf_v[j].at[c, rows(i1 * 256 + i2 * 64 + z * 32, 32)]
         mine[...] = value.astype(BF16)
         for di, dz in EIGHT:
-            send(mine, mine, ("all8", j), ("all8", j), (eight(di, dz), mp))
+            send(mine, mine, "all8", ("all8", j), (eight(di, dz), mp))
 
     def to_core(j, i):
         block = cf_v[j].at[c, rows(quarter1(i), 256)]
-        send(block, block, ("core", j), ("core", j), (other_core, mp))
+        send(block, block, "core", ("core", j), (other_core, mp))
 
     def gather(j):
         buf = cf_v[j].at[c]
         recv(("all8", j), buf.at[rows(quarter1(i1), 224)])
         block = buf.at[rows(quarter1(i1), 256)]
         for device in (right1, left1) + ((opposite1,) if CHUNKS[j][2] else ()):
-            send(block, block, ("four", j), ("begin", j), (device, mp))
+            send(block, block, "four", ("begin", j), (device, mp))
         to_core(j, i1)
 
     def forward(j):
         buf = cf_v[j].at[c]
         recv(("begin", j), buf.at[0:512])
         half = buf.at[part(i1 + 3, 0)]
-        send(half, half, ("four", j), ("forward", j), (right1, mp))
+        send(half, half, "four", ("forward", j), (right1, mp))
         half = buf.at[part(i1 + 1, 1)]
-        send(half, half, ("four", j), ("forward", j), (left1, mp))
+        send(half, half, "four", ("forward", j), (left1, mp))
         to_core(j, i1 + 3)
         to_core(j, i1 + 1)
 
@@ -360,13 +360,13 @@
         gram = lr_v[0].astype(F32) + lr_v[1].astype(F32) + lr_v[2].astype(F32) + lr_v[3].astype(F32)
         left_out[...] = 0.9 * left_v[...] + 0.1 * (gram / (4 * COLS))
     with jax.named_scope("sent"):
-        for j in range(len(CHUNKS)):
-            wait_sent(("pair", j), p_v[j])
-            wait_sent(("ring", j), r1_v[j])
-            wait_sent(("eight", j), r2_v[j])
-            wait_sent(("all8", j), cf_v[j].at[0, 0:224])
-            wait_sent(("four", j), cf_v[j].at[0, 0:768])
-            wait_sent(("core", j), cf_v[j].at[0])
+        for n in range(2):
+            wait_sent(("pair", n), a_v)
+            wait_sent(("ring", n), a_v.at[0:768])
+        wait_sent("eight", a_v.at[0:448])
+        wait_sent("all8", a_v.at[0:224])
+        wait_sent("four", a_v.at[0:768])
+        wait_sent("core", a_v)
         wait_sent("basis", bp_v.at[0, 0:480])
         for name in ("basis_core", "basis_z", "basis_forward"):
             wait_sent(name, bp_v.at[0])

time: 65.8 us -> 65.2 us (level)
  no operation moved by 1% of the time
where the time goes in v5:
time: 65.2 us; the launch traced here: 65.1 us
  Pallas kernels  64.4 us (99%)
    pallas_call x1, Pallas kernels, body(): pl.pallas_call(kernel, out_shape=tuple((pltpu.VMEM(q.shape, q.dtype) for...  63.7 us

profile of v5, /device:TPU:1, one launch (start us, length us, event | category | flops | bytes accessed | tf_op | source)
XLA Modules:
  0.0 65.1 jit_solution(14310909494034753383)
XLA Ops:
  0.6 63.7 %shard_map.76 = (f32[16,1024]{1,0:T(8,128)S(1)}, f32[1,32,2048]{2,1,0:T(8,128)S(1)}, bf16[16,2048]{1,0:T(8,128)(2,1)S(1)}) custom-call(bf16[1024,1024]{1,0:T(8,128)(2,1)} %a_hbm.1, bf16[1024,2048]{1,0:T(8,128)(2,1)} %g_hbm.1, f32[16,1024]{1,0:T(8,128)} %left_hbm.1, f32[1,32,2048]{2,1,0:T(8,128)} %right_hbm.1, bf16[1,32,2048]{2,1,0:T(8,128)(2,1)} %basis_hbm.1), custom_call_target="tpu_custom_call" | custom-call | flops 5000000000 | bytes 7340032 | tf_op jit(solution)/shard_map/pallas_call | solution.py:401
  64.3 0.8 %shard_map.77 = (f32[16,1024]{1,0:T(8,128)}, f32[1,32,2048]{2,1,0:T(8,128)}, bf16[16,2048]{1,0:T(8,128)(2,1)}) custom-call(f32[16,1024]{1,0:T(8,128)S(1)} %get-tuple-element.6.refs_0_, f32[1,32,2048]{2,1,0:T(8,128)S(1)} %get-tuple-element.7.refs_1_, bf16[16,2048]{1,0:T(8,128)(2,1)S(1)} %get-tuple-element.8.refs_2_), custom_call_target="tpu_custom_call" | custom-call | tf_op jit(solution)/shard_map/pallas_call | solution.py:434
